TPU v7x, 128 devices: a whole 4x4x4 slice. The times are simulated.
128 devices in a mesh: section: 2 (over core), peer: 64 (over y, x, z).
Axes of the slice: x: 4, y: 4, z: 4, core: 2. Of those that a mesh axis runs over, the one named last changes fastest.
Arguments:
- inputs: bfloat16 [8192, 5120], P('peer'), may hold values from -6 to 6
- routes: int32 [8192, 1], P('peer'), may hold values from 0 to 63; in each aligned block of 128 rows (0 to 127, 128 to 255, ...) at most 4 rows name the same one
- counts: int32 [64], P('peer'), may hold values from 96 to 128, as said below
- cotangent: bfloat16 [64, 256, 5120], P('peer'), may hold values from -6 to 6
- gain_vector: float32 [2, 5120], P('section'), may hold values from 0.1 to 1.9
- w_down: bfloat16 [2, 5120, 256], P('section'), may hold values from -0.078125 to 0.078125
- w_up: bfloat16 [2, 256, 5120], P('section'), may hold values from -0.375 to 0.375
Outputs:
- grad_gain: bfloat16 [2, 5120], P('section')
- grad_down: bfloat16 [2, 5120, 256], P('section')
- grad_up: bfloat16 [2, 256, 5120], P('section')
- row_grads: bfloat16 [2, 8192, 5120], P('section', 'peer')
Inputs may be any that keep to these rules, and one draw needn't show every extreme that they name: `routes`: in the 128 rows of each first-section peer, no destination is named by more than 4 rows, and one is named by exactly 4. `counts`: some peer has all 128 rows live.
All inputs are finite; a program needn't handle non-finite values.
Results may differ from a plain program's by a relative error of at most 0.009.
Values may be sent and summed in bfloat16 or wider, within the bound.
A program may use at most 128 MiB of HBM per device.

v0:
```python
import jax
import jax.numpy as jnp
from jax import lax
from jax.sharding import PartitionSpec as P

rms_eps = 1e-05


def layer_forward(rows_in, gain_vec, down_w, up_w):
    x_float = rows_in.astype(jnp.float32)
    inv_rms = lax.rsqrt(jnp.mean(x_float * x_float, axis=-1, keepdims=True) + rms_eps)
    x_hat = x_float * inv_rms
    normed = (x_hat * gain_vec).astype(jnp.bfloat16)
    hidden = jnp.dot(normed, down_w, preferred_element_type=jnp.float32)
    active = jax.nn.silu(hidden).astype(jnp.bfloat16)
    result = (x_float + jnp.dot(active, up_w, preferred_element_type=jnp.float32)).astype(
        jnp.bfloat16
    )
    return (result, (x_hat, inv_rms, normed, hidden, active))


def layer_backward(saved_state, grad_out, gain_vec, down_w, up_w):
    x_hat, inv_rms, normed, hidden, active = saved_state
    outer = (((0,), (0,)), ((), ()))
    inner = (((1,), (1,)), ((), ()))
    g_up = lax.dot_general(active, grad_out, outer, preferred_element_type=jnp.float32)
    d_active = lax.dot_general(grad_out, up_w, inner, preferred_element_type=jnp.float32)
    gate_sig = jax.nn.sigmoid(hidden)
    d_hidden = (d_active * gate_sig * (1.0 + hidden * (1.0 - gate_sig))).astype(jnp.bfloat16)
    g_down = lax.dot_general(normed, d_hidden, outer, preferred_element_type=jnp.float32)
    d_normed = lax.dot_general(d_hidden, down_w, inner, preferred_element_type=jnp.float32)
    g_gain = jnp.sum(d_normed * x_hat, axis=0)
    d_hat = d_normed * gain_vec
    d_input = grad_out.astype(jnp.float32) + inv_rms * (
        d_hat - x_hat * jnp.mean(d_hat * x_hat, axis=-1, keepdims=True)
    )
    return ((g_gain, g_down, g_up), d_input.astype(jnp.bfloat16))


def zero_grads(feature_dim, bottleneck):
    return (
        jnp.zeros((feature_dim,), jnp.float32),
        jnp.zeros((feature_dim, bottleneck), jnp.float32),
        jnp.zeros((bottleneck, feature_dim), jnp.float32),
    )


def shards(inputs, routes, counts, cotangent, gain_vector, w_down, w_up):
    n_peer = lax.axis_size("peer")
    row_count = inputs.shape[0]
    feature_dim = inputs.shape[1]
    bottleneck = w_down.shape[2]
    slot_total = cotangent.shape[1]
    capacity = slot_total // n_peer
    section_idx = lax.axis_index("section")
    gain_own = gain_vector[0]
    down_own = w_down[0]
    up_own = w_up[0]
    dest_peer = routes[:, 0]
    row_ids = jnp.arange(row_count, dtype=jnp.int32)
    live_rows = row_ids < counts[0]
    one_hot = (
        (dest_peer[:, None] == jnp.arange(n_peer, dtype=jnp.int32)[None, :]) & live_rows[:, None]
    ).astype(jnp.int32)
    row_ranks = jnp.cumsum(one_hot, axis=0) - 1
    slot_index = jnp.sum(one_hot * row_ranks, axis=1)
    flat_slot = jnp.where(live_rows, dest_peer * capacity + slot_index, slot_total)
    source_row = (
        jnp.full((slot_total,), row_count, jnp.int32).at[flat_slot].set(row_ids, mode="drop")
    )

    def first_forward():
        return layer_forward(inputs, gain_own, down_own, up_own)

    def spare_forward():
        return (
            jnp.zeros((row_count, feature_dim), jnp.bfloat16),
            (
                jnp.zeros((row_count, feature_dim), jnp.float32),
                jnp.zeros((row_count, 1), jnp.float32),
                jnp.zeros((row_count, feature_dim), jnp.bfloat16),
                jnp.zeros((row_count, bottleneck), jnp.float32),
                jnp.zeros((row_count, bottleneck), jnp.bfloat16),
            ),
        )

    first_out, saved_first = lax.cond(section_idx == 0, first_forward, spare_forward)
    outgoing = jnp.take(first_out, source_row, axis=0, mode="fill", fill_value=0).reshape(
        n_peer, capacity, feature_dim
    )
    padded = jnp.concatenate([jnp.zeros_like(outgoing), outgoing], axis=0)
    arrived = lax.all_to_all(padded, ("section", "peer"), split_axis=0, concat_axis=0, tiled=True)[
        :n_peer
    ]
    slots_in = arrived.reshape(slot_total, feature_dim)

    def second_pass():
        second_out, saved_second = layer_forward(slots_in, gain_own, down_own, up_own)
        return layer_backward(saved_second, cotangent[0], gain_own, down_own, up_own)

    def spare_second():
        return (
            zero_grads(feature_dim, bottleneck),
            jnp.zeros((slot_total, feature_dim), jnp.bfloat16),
        )

    grads_second, back_slots = lax.cond(section_idx == 1, second_pass, spare_second)
    back_slots = back_slots.reshape(n_peer, capacity, feature_dim)
    doubled = jnp.concatenate([back_slots, back_slots], axis=0)
    returned = lax.all_to_all(
        doubled, ("section", "peer"), split_axis=0, concat_axis=0, tiled=True
    )[n_peer:]
    grad_rows = jnp.take(
        returned.reshape(slot_total, feature_dim), flat_slot, axis=0, mode="fill", fill_value=0
    )

    def first_backward():
        return layer_backward(saved_first, grad_rows, gain_own, down_own, up_own)

    def spare_backward():
        return (
            zero_grads(feature_dim, bottleneck),
            jnp.zeros((row_count, feature_dim), jnp.bfloat16),
        )

    grads_first, in_rows = lax.cond(section_idx == 0, first_backward, spare_backward)
    row_block = jnp.where(section_idx == 0, in_rows, grad_rows)[None]
    own_grads = jax.tree.map(lambda a, b: a + b, grads_first, grads_second)
    factor = float(row_count * n_peer) ** (-0.5)
    summed = lax.psum((own_grads[0], own_grads[1], own_grads[2]), "peer")
    return (
        (summed[0] * factor).astype(jnp.bfloat16)[None],
        (summed[1] * factor).astype(jnp.bfloat16)[None],
        (summed[2] * factor).astype(jnp.bfloat16)[None],
        row_block,
    )


def solution(mesh):
    in_specs = (
        P("peer", None),
        P("peer", None),
        P("peer"),
        P("peer", None, None),
        P("section", None),
        P("section", None, None),
        P("section", None, None),
    )
    out_specs = (
        P("section", None),
        P("section", None, None),
        P("section", None, None),
        P("section", "peer", None),
    )
    return jax.shard_map(shards, mesh=mesh, in_specs=in_specs, out_specs=out_specs, check_vma=False)
```

profile of v0, /device:TPU:0, one launch (start us, length us, event | category | flops | bytes accessed | tf_op | source)
XLA Modules:
  0.0 640.2 jit_solution(8514418773213489420)
XLA Ops:
  7.8 0.8 fusion.25
  8.6 0.2 reduce_window_sum.11
  8.8 0.8 select_reduce_fusion
  9.6 0.7 and_bitcast_fusion
  10.3 1.0 scatter_custom_fusion
  11.3 0.1 broadcast_in_dim.54
  11.4 9.7 %conditional.3 = (bf16[128,5120]{1,0:T(8,128)(2,1)S(1)}, f32[128,5120]{1,0:T(8,128)}, f32[128,1]{0,1:T(1,128)S(1)}, bf16[128,5120]{1,0:T(8,128)(2,1)}, f32[128,256]{1,0:T(8,128)S(1)}, /*index=5*/bf16[128,256]{1,0:T(8,128)(2,1)}) conditional(s32[]{:T(128)} %convert_element_type.64, () %tuple.34, (bf16[128,5120]{1,0:T(8,128)(2,1)}, ...), branch_computations={%region_0.0_spmd, %region_1.3_spmd} | conditional | flops 677806208 | bytes 42228356 | solution.py:87
  11.4 1.7 fusion.1
  13.1 0.0 copy-start.2
  13.1 3.9 multiply_convert_fusion
  17.0 0.0 copy-done.2
  17.0 2.7 multiply_convert_fusion.1
  19.7 1.4 fusion
  21.1 3.6 gather_fusion
  24.6 4.2 gather.11
  28.9 1.2 broadcast_select_fusion
  30.1 4.0 concatenate.6
  34.1 11.6 %all-to-all-start = ((bf16[128,4,5120]{2,1,0:T(4,128)(2,1)}), bf16[128,4,5120]{2,1,0:T(4,128)(2,1)}, u32[]{:S(2)}, u32[]{:S(2)}) async-start(bf16[128,4,5120]{2,1,0:T(4,128)(2,1)} %concatenate.6), calls=%async_computation | async-start | bytes 10485760 | tf_op jit(solution)/shard_map/all_to_all | solution.py:92
  45.7 63.0 %all-to-all-done = bf16[128,4,5120]{2,1,0:T(4,128)(2,1)} async-done(((bf16[128,4,5120]{2,1,0:T(4,128)(2,1)}), bf16[128,4,5120]{2,1,0:T(4,128)(2,1)}, u32[]{:S(2)}, u32[]{:S(2)}) %all-to-all-start) | async-done | bytes 5242912 | tf_op jit(solution)/shard_map/all_to_all | solution.py:92
  108.7 7.4 %conditional.4 = (f32[5120]{0:T(1024)S(1)}, f32[5120,256]{1,0:T(8,128)}, f32[256,5120]{1,0:T(8,128)}, bf16[256,5120]{1,0:T(8,128)(2,1)}) conditional(s32[]{:T(128)} %convert_element_type.66, () %tuple.33, (bf16[1,256,5120]{2,1,0:T(8,128)(2,1)}, bf16[256,5120]{1,0:T(8,128)(2,1)}, bf16[128,4,5120]{2,1,0:T(4,128)(2,1)}, f32[1,5120]{1,0:T(1,128)S(1)}, ...), branch_computations={%region_6.7_spmd, %region_7.11_spmd} | conditional | flops 3387813120 | bytes 119260296 | solution.py:107
  108.7 1.8 broadcast.136
  110.5 2.9 broadcast.135
  113.4 2.7 broadcast.134
  116.1 4.2 reshape.89
  120.4 5.7 pad_maximum_fusion
  126.1 36.2 %all-to-all-start.1 = ((bf16[128,4,5120]{2,1,0:T(4,128)(2,1)}), bf16[128,4,5120]{2,1,0:T(4,128)(2,1)}, u32[]{:S(2)}, u32[]{:S(2)}) async-start(bf16[128,4,5120]{2,1,0:T(4,128)(2,1)} %pad_maximum_fusion), calls=%async_computation.1 | async-start | bytes 10485760 | tf_op jit(solution)/shard_map/all_to_all | solution.py:110
  162.2 0.0 all-reduce.4.cloned.1.call-start
  162.3 62.9 %all-to-all-done.1 = bf16[128,4,5120]{2,1,0:T(4,128)(2,1)} async-done(((bf16[128,4,5120]{2,1,0:T(4,128)(2,1)}), bf16[128,4,5120]{2,1,0:T(4,128)(2,1)}, u32[]{:S(2)}, u32[]{:S(2)}) %all-to-all-start.1) | async-done | bytes 5242912 | tf_op jit(solution)/shard_map/all_to_all | solution.py:110
  225.2 4.1 slice.12
  229.3 4.0 reshape.90
  233.4 2.4 gather_fusion.1
  235.8 1.6 broadcast_select_fusion.1
  237.4 0.5 copy-done.1
  237.9 22.5 %conditional.5 = (f32[5120]{0:T(1024)S(1)}, f32[256,5120]{1,0:T(8,128)}, bf16[128,5120]{1,0:T(8,128)(2,1)S(1)}, f32[5120,256]{1,0:T(8,128)}) conditional(s32[]{:T(128)} %convert_element_type.64, () %tuple.32, (bf16[128,5120]{1,0:T(8,128)(2,1)S(1)}, bf16[256,5120]{1,0:T(8,128)(2,1)}, f32[128,256]{1,0:T(8,128)S(1)}, ...), branch_computations={%region_11.12_spmd, %region_12.15_spmd} | conditional | flops 1350331392 | bytes 43711008 | solution.py:126
  237.9 2.7 fusion.21
  240.6 2.9 multiply_reduce_fusion.3
  243.5 2.5 add_convert_fusion.1
  246.0 4.0 fusion.28
  250.0 4.5 convolution_bitcast_fusion
  254.5 6.0 copy.16
  260.4 7.2 %add.93 = f32[256,5120]{1,0:T(8,128)} add(f32[256,5120]{1,0:T(8,128)} %get-tuple-element.85, f32[256,5120]{1,0:T(8,128)} %get-tuple-element.86) | non-fusion elementwise | flops 1310720 | bytes 15728640 | tf_op jit(solution)/shard_map/add | solution.py:128
  267.6 7.1 %add.92 = f32[5120,256]{1,0:T(8,128)} add(f32[5120,256]{1,0:T(8,128)} %get-tuple-element.92, f32[5120,256]{1,0:T(8,128)} %get-tuple-element.84) | non-fusion elementwise | flops 1310720 | bytes 15728640 | tf_op jit(solution)/shard_map/add | solution.py:128
  274.7 0.0 all-reduce.4.cloned.1.call-update
  274.7 350.1 %psum.21 = f32[5120]{0:T(1024)S(1)} all-reduce(f32[5120]{0:T(1024)S(1)} %add.91), channel_id=1, replica_groups=mesh['section'=2,'peer'=64] {'peer'}, use_global_device_ids=true, to_apply=%region_15.16 | all-reduce | flops 5120 | bytes 40960 | tf_op jit(solution)/shard_map/psum | solution.py:130
  624.8 0.6 broadcast_in_dim.59
  625.4 1.3 select_bitcast_fusion
  626.7 4.7 fusion.22
  631.4 2.0 fusion.23
  (25 shorter events, 0.1 us)
Async XLA Ops:
  13.1 3.9 copy-start.2
  17.0 2.7 copy-start.4
  17.0 2.7 copy-start.5
  34.1 74.6 %copy-start = (bf16[1,5120,256]{2,1,0:T(8,128)(2,1)S(1)}, bf16[1,5120,256]{2,1,0:T(8,128)(2,1)}, u32[]{:S(2)}) copy-start(bf16[1,5120,256]{2,1,0:T(8,128)(2,1)} %param.18) | copy-start | bytes 7864324
  34.1 74.6 %copy-start.9 = (f32[1,5120]{1,0:T(1,128)S(1)}, f32[1,5120]{1,0:T(1,128)}, u32[]{:S(2)}) copy-start(f32[1,5120]{1,0:T(1,128)} %param.17) | copy-start | bytes 61444
  34.1 74.6 %all-to-all-start = ((bf16[128,4,5120]{2,1,0:T(4,128)(2,1)}), bf16[128,4,5120]{2,1,0:T(4,128)(2,1)}, u32[]{:S(2)}, u32[]{:S(2)}) async-start(bf16[128,4,5120]{2,1,0:T(4,128)(2,1)} %concatenate.6), calls=%async_computation | async-start | bytes 10485760 | tf_op jit(solution)/shard_map/all_to_all | solution.py:92
  126.1 99.2 %all-to-all-start.1 = ((bf16[128,4,5120]{2,1,0:T(4,128)(2,1)}), bf16[128,4,5120]{2,1,0:T(4,128)(2,1)}, u32[]{:S(2)}, u32[]{:S(2)}) async-start(bf16[128,4,5120]{2,1,0:T(4,128)(2,1)} %pad_maximum_fusion), calls=%async_computation.1 | async-start | bytes 10485760 | tf_op jit(solution)/shard_map/all_to_all | solution.py:110
  162.2 464.5 %all-reduce.4.cloned.1.call-start = ((), (), s32[]{:S(2)}) async-start(), calls=%async_computation.2 | async-start | bytes 20971520 | tf_op jit(solution)/shard_map/psum | solution.py:130
  235.8 2.1 copy-start.1
  274.6 350.8 %copy-start.3 = (bf16[128,5120]{1,0:T(8,128)(2,1)S(1)}, bf16[128,5120]{1,0:T(8,128)(2,1)}, u32[]{:S(2)}) copy-start(bf16[128,5120]{1,0:T(8,128)(2,1)} %gather_fusion.1) | copy-start | bytes 3932164
  626.7 4.7 copy-start.8
Sparse Core Ops, SparseCore 0:
  274.8 182.1 all-reduce.3
where the time goes:
time: 641 us; the launch traced here: 640 us
  blocking collectives  350 us (55%)
  waiting for transfers between devices  126 us (20%)
  starting transfers between devices  47.8 us (7%)
  local copies, waits for them, and re-layouts  42.2 us (7%)
  other arithmetic  41.1 us (6%)
  matrix products  18.2 us (3%)
  between operations  14.8 us (2%)
    psum x1, blocking collectives, shards(): summed = lax.psum((own_grads[0], own_grads[1], own_grads[2]), 'peer')  350 us
    all_to_all x1, waiting for transfers between devices, shards(): lax.all_to_all(padded, ('section', 'peer'), split_axis=0, concat_axis=0,...  63 us
    all_to_all x1, waiting for transfers between devices, shards(): lax.all_to_all(doubled, ('section', 'peer'), split_axis=0, concat_axis=0,...  62.9 us
    all_to_all x1, starting transfers between devices, shards(): lax.all_to_all(doubled, ('section', 'peer'), split_axis=0, concat_axis=0,...  36.2 us
    add x3, other arithmetic, shards(): own_grads = jax.tree.map(lambda a, b: a + b, grads_first, grads_second)  14.2 us
  transfers between devices with their start and end apart: 3, of which 2 were waited for; matrix products, arithmetic and copies ran while one was open for 0% of the time, Pallas kernels for 0%

commit v1 on v0

v1 whole, which is shorter than its diff:
```python
import jax
import jax.numpy as jnp
from jax import lax
from jax.experimental import pallas as pl
from jax.experimental.pallas import tpu as pltpu
from jax.sharding import PartitionSpec as P

rms_eps = 1e-05
MESH = pl.DeviceIdType.MESH
BF = jnp.bfloat16
F32 = jnp.float32

ROWS, D, R = 128, 5120, 256
SLOTS, CAP = 256, 4
N_PEER, RING = 64, 4
HALF = D // 2
QUART = HALF // 4
CH = 640
N_CH = D // CH
ACOL = D // RING
UP_OFF, UP_W = (0, 384, 768), (384, 384, 512)
DN_OFF, DN_H = (0, 32, 64), (32, 32, 16)
ORDER = ((0, 1, 2), (1, 2, 0), (2, 0, 1))
FACTOR = float(N_PEER * ROWS) ** (-0.5)
INNER = (((1,), (1,)), ((), ()))


def mod4(v):
    return lax.rem(v + 8, 4)


def rcopy(src, dst, send_sem, recv_sem, device):
    return pltpu.make_async_remote_copy(
        src_ref=src,
        dst_ref=dst,
        send_sem=send_sem,
        recv_sem=recv_sem,
        device_id=device,
        device_id_type=MESH,
    )


def wait_recv(dst, sems, device):
    rcopy(dst, dst, sems[0], sems[1], device).wait_recv()


def wait_send(src, sems, device):
    rcopy(src, src, sems[0], sems[1], device).wait_send()


def kernel(
    x_hbm, routes_ref, counts_ref, cot_hbm, gain_ref, wd_hbm, wu_hbm,
    out_gain, out_dn, out_up, out_rows,
    x_v, wd_v, wu_v, cot_v, a2a_send, a2a_recv, nt, cv, fo, sel, act_t,
    gu0, gu1, gu2, gd0, gd1, gd2,
    ru0, ru1, ru2, rd0, rd1, rd2,
    iu0, iu1, iu2, id0, id1, id2,
    su0, su1, su2, sd0, sd1, sd2,
    i2u0, i2u1, i2u2, i2d0, i2d1, i2d2,
    s2u0, s2u1, s2u2, s2d0, s2d1, s2d2,
    i3u0, i3u1, i3u2, i3d0, i3d1, i3d2,
    gg, gin,
    load_sem, own_sem, a2a_ssem, a2a_rsem, row_ssem, row_rsem, red_ssem, red_rsem, gain_ssem, gain_rsem,
):
    grad = ((gu0, gu1, gu2), (gd0, gd1, gd2))
    rly = ((ru0, ru1, ru2), (rd0, rd1, rd2))
    inb = ((iu0, iu1, iu2), (id0, id1, id2))
    s1 = ((su0, su1, su2), (sd0, sd1, sd2))
    in2 = ((i2u0, i2u1, i2u2), (i2d0, i2d1, i2d2))
    s2 = ((s2u0, s2u1, s2u2), (s2d0, s2d1, s2d2))
    in3 = ((i3u0, i3u1, i3u2), (i3d0, i3d1, i3d2))

    sec = lax.axis_index("section")
    me = lax.axis_index("peer")
    pos = (me // 16, lax.rem(me // 4, 4), lax.rem(me, 4))
    weight = (16, 4, 1)

    def along(axis, step):
        there = mod4(pos[axis] + step)
        return (sec, me + (there - pos[axis]) * weight[axis])

    partner = (1 - sec, me)

    cot_load = pltpu.make_async_copy(
        cot_hbm.at[0, :, pl.ds(pl.multiple_of(sec * HALF, HALF), HALF)], cot_v, load_sem.at[0]
    )
    wd_load = pltpu.make_async_copy(wd_hbm.at[0], wd_v, load_sem.at[1])
    wu_load = pltpu.make_async_copy(wu_hbm.at[0], wu_v, load_sem.at[2])
    x_load = pltpu.make_async_copy(x_hbm, x_v, load_sem.at[3])
    cot_load.start()

    @pl.when(sec == 0)
    def _():
        x_load.start()

    wd_load.start()
    wu_load.start()

    barrier = pltpu.get_barrier_semaphore()

    @pl.when(sec == 0)
    def _():
        pl.semaphore_signal(barrier, inc=1, device_id=partner, device_id_type=MESH)
        for axis in range(3):
            for step in range(1, 4):
                pl.semaphore_signal(barrier, inc=1, device_id=along(axis, step), device_id_type=MESH)

    @pl.when(sec == 1)
    def _():
        def greet(i, carry):
            pl.semaphore_signal(
                barrier, inc=1, device_id=(sec, lax.rem(me + i, N_PEER)), device_id_type=MESH
            )
            return carry

        lax.fori_loop(1, N_PEER, greet, 0)

    cot_load.wait()
    o_i = lax.broadcasted_iota(jnp.int32, (SLOTS, SLOTS), 0)
    i_i = lax.broadcasted_iota(jnp.int32, (SLOTS, SLOTS), 1)
    perm = jnp.where(i_i == (o_i & 3) * 64 + (o_i >> 2), 1.0, 0.0).astype(BF)

    def arrange(g, carry):
        rows = pl.ds(pl.multiple_of(g * 64, 64), 64)
        block = jnp.concatenate(
            [cot_v[rows, j * QUART:(j + 1) * QUART] for j in range(4)], axis=0
        )
        moved = jnp.dot(perm, block, preferred_element_type=F32).astype(BF)
        a2a_send[pl.ds(pl.multiple_of(g * 16, 16), 16)] = moved.reshape(16, 16, QUART)
        return carry

    lax.fori_loop(0, 4, arrange, 0)

    @pl.when(sec == 0)
    def _():
        pl.semaphore_wait(barrier, 10)

        def send(i, carry):
            dst = lax.rem(me + i * 21, N_PEER)
            rcopy(
                a2a_send.at[dst], a2a_recv.at[0, me], a2a_ssem, a2a_rsem.at[0], (1, dst)
            ).start()
            return carry

        lax.fori_loop(0, N_PEER, send, 0)

    @pl.when(sec == 1)
    def _():
        pl.semaphore_wait(barrier, N_PEER)
        pl.semaphore_signal(barrier, inc=1, device_id=partner, device_id_type=MESH)
        pltpu.make_async_copy(a2a_send.at[me], a2a_recv.at[1, me], own_sem).start()

        def send(i, carry):
            dst = lax.rem(me + i * 21, N_PEER)
            rcopy(
                a2a_send.at[dst], a2a_recv.at[1, me], a2a_ssem, a2a_rsem.at[1], (1, dst)
            ).start()
            return carry

        lax.fori_loop(1, N_PEER, send, 0)

    def cols_of(c):
        return pl.ds(pl.multiple_of(c * CH, CH), CH)

    def row_wait(ref, c):
        return rcopy(ref.at[:, cols_of(c)], ref.at[:, cols_of(c)], row_ssem.at[c], row_rsem.at[c], partner)

    @pl.when(sec == 0)
    def _():
        x_load.wait()

    def squares(c, total):
        @pl.when(sec == 1)
        def _():
            row_wait(x_v, c).wait_recv()

        xf = x_v[:, cols_of(c)].astype(F32)
        return total + jnp.sum(xf * xf, axis=1, keepdims=True)

    total = lax.fori_loop(0, N_CH, squares, jnp.zeros((ROWS, 1), F32))
    inv = lax.rsqrt(total / D + rms_eps)
    wd_load.wait()

    def down(c, hidden):
        xf = x_v[:, cols_of(c)].astype(F32)
        normed = (xf * inv * gain_ref[:, cols_of(c)]).astype(BF)
        nt[c // 2, pl.ds(pl.multiple_of(lax.rem(c, 2) * 8, 8), 8)] = normed.T.reshape(8, 80, ROWS)
        return hidden + jnp.dot(normed, wd_v[cols_of(c), :], preferred_element_type=F32)

    hidden = lax.fori_loop(0, N_CH, down, jnp.zeros((ROWS, R), F32))
    gate = jax.nn.sigmoid(hidden)
    active = (hidden * gate).astype(BF)
    act_t[...] = active.T
    wu_load.wait()

    @pl.when(sec == 0)
    def _():
        def up(c, carry):
            y = jnp.dot(active, wu_v[:, cols_of(c)], preferred_element_type=F32)
            fo[:, cols_of(c)] = (x_v[:, cols_of(c)].astype(F32) + y).astype(BF)
            rcopy(
                fo.at[:, cols_of(c)], x_v.at[:, cols_of(c)], row_ssem.at[c], row_rsem.at[c], partner
            ).start()
            return carry

        lax.fori_loop(0, N_CH, up, 0)

    @pl.when(sec == 1)
    def _():
        dest = routes_ref[...]
        live = lax.broadcasted_iota(jnp.int32, (ROWS, 1), 0) < counts_ref[...]
        lane = lax.broadcasted_iota(jnp.int32, (ROWS, ROWS), 1)
        row = lax.broadcasted_iota(jnp.int32, (ROWS, ROWS), 0)
        named = jnp.where((lane == dest) & live, 1.0, 0.0)
        before = jnp.where(lane < row, 1.0, 0.0).astype(BF)
        rank = jnp.dot(before, named.astype(BF), preferred_element_type=F32)
        nth = jnp.sum(named * rank, axis=1, keepdims=True)
        place = jnp.where(live, dest.astype(F32) * 16.0 + nth * 4.0, -16.0)
        column = lax.broadcasted_iota(jnp.int32, (ROWS, N_PEER * 16), 1).astype(F32)
        for j in range(4):
            sel[j * ROWS:(j + 1) * ROWS, :] = jnp.where(column == place + float(j), 1.0, 0.0).astype(BF)
        for h in range(2):
            if h == 0:
                rcopy(a2a_recv.at[0], a2a_recv.at[0], a2a_ssem, a2a_rsem.at[0], partner).wait_recv()
            else:
                pltpu.make_async_copy(a2a_send.at[me], a2a_recv.at[1, me], own_sem).wait()
                rest = a2a_recv.at[1, pl.ds(0, N_PEER - 1)]
                rcopy(rest, rest, a2a_ssem, a2a_rsem.at[1], partner).wait_recv()
            for n in range(QUART // 128):
                block = a2a_recv[h, :, :, n * 128:(n + 1) * 128].reshape(N_PEER * 16, 128)
                picked = jnp.dot(sel[...], block, preferred_element_type=F32).astype(BF)
                for j in range(4):
                    lo = h * HALF + j * QUART + n * 128
                    cv[:, lo:lo + 128] = picked[j * ROWS:(j + 1) * ROWS, :]

    def out_at(t, k, a, b, c):
        if t == 0:
            cols = pl.ds(pl.multiple_of(a * ACOL + UP_OFF[k], 128), UP_W[k])
            return out_up.at[b, c, :, cols]
        return out_dn.at[a, b, c, pl.ds(DN_OFF[k], DN_H[k]), :]

    every = pl.ds(0, RING)
    lower, upper = pl.ds(0, 2), pl.ds(2, 2)

    def sems(t, k, i):
        return red_ssem.at[t, k, i], red_rsem.at[t, k, i]

    def ship(src, dst, t, k, i, device):
        rcopy(src, dst, *sems(t, k, i), device).start()

    def here(dst, t, k, i, device):
        wait_recv(dst, sems(t, k, i), device)

    def first_axis(k):
        return pos[ORDER[k][0]]

    def sides(k):
        axis = ORDER[k][0]
        return along(axis, -1), along(axis, 1)

    def stage1_send(t):
        for k in range(3):
            g, left, right = grad[t][k], *sides(k)
            ship(g.at[2, lower], rly[t][k].at[0], t, k, 0, right)
            ship(g.at[2, upper], rly[t][k].at[1], t, k, 1, left)
            ship(g.at[1, upper], inb[t][k].at[0, upper], t, k, 2, right)
            ship(g.at[3, lower], inb[t][k].at[1, lower], t, k, 3, left)

    def stage1_merge(t):
        for k in range(3):
            g, left, right = grad[t][k], *sides(k)
            here(rly[t][k].at[0], t, k, 0, left)
            g[1, 0:2] = (g[1, 0:2].astype(F32) + rly[t][k][0].astype(F32)).astype(BF)
            ship(g.at[1, lower], inb[t][k].at[0, lower], t, k, 4, right)
            here(rly[t][k].at[1], t, k, 1, right)
            g[3, 2:4] = (g[3, 2:4].astype(F32) + rly[t][k][1].astype(F32)).astype(BF)
            ship(g.at[3, upper], inb[t][k].at[1, upper], t, k, 5, left)

    def stage2_send(t):
        for k in range(3):
            g, left, right = grad[t][k], *sides(k)
            box, part = inb[t][k], s1[t][k]
            here(box.at[0, upper], t, k, 2, left)
            here(box.at[1, lower], t, k, 3, right)
            here(box.at[0, lower], t, k, 4, left)
            here(box.at[1, upper], t, k, 5, right)

            def add(b, carry, g=g, box=box, part=part):
                part[b] = (g[0, b].astype(F32) + box[0, b].astype(F32) + box[1, b].astype(F32)).astype(BF)
                return carry

            lax.fori_loop(0, RING, add, 0)
            axis = ORDER[k][1]
            for step in range(1, 4):
                ship(part.at[mod4(pos[axis] + step)], in2[t][k].at[step - 1], t, k, 5 + step, along(axis, step))

    def stage3_send(t):
        for k in range(3):
            axis = ORDER[k][1]
            box, part = in2[t][k], s2[t][k]
            for step in range(1, 4):
                here(box.at[step - 1], t, k, 5 + step, along(axis, -step))
            mine = s1[t][k][pos[axis]].astype(F32)
            part[...] = (mine + box[0].astype(F32) + box[1].astype(F32) + box[2].astype(F32)).astype(BF)
            axis = ORDER[k][2]
            for step in range(1, 4):
                ship(part.at[mod4(pos[axis] + step)], in3[t][k].at[step - 1], t, k, 8 + step, along(axis, step))

    def gather1_send(t):
        for k in range(3):
            a, b, c = (pos[axis] for axis in ORDER[k])
            axis = ORDER[k][2]
            box = in3[t][k]
            for step in range(1, 4):
                here(box.at[step - 1], t, k, 8 + step, along(axis, -step))
            mine = s2[t][k][c].astype(F32)
            whole = mine + box[0].astype(F32) + box[1].astype(F32) + box[2].astype(F32)
            piece = out_at(t, k, a, b, c)
            piece[...] = (whole * FACTOR).astype(BF)
            for step in range(1, 4):
                ship(piece, piece, t, k, 11 + step, along(axis, step))

    def gather2_send(t):
        for k in range(3):
            a, b, c = (pos[axis] for axis in ORDER[k])
            axis = ORDER[k][2]
            for step in range(1, 4):
                here(out_at(t, k, a, b, mod4(c - step)), t, k, 11 + step, along(axis, -step))
            axis = ORDER[k][1]
            line = out_at(t, k, a, b, every)
            for step in range(1, 4):
                ship(line, line, t, k, 14 + step, along(axis, step))

    def gather3_send(t):
        for k in range(3):
            a, b, c = (pos[axis] for axis in ORDER[k])
            axis = ORDER[k][1]
            for step in range(1, 4):
                here(out_at(t, k, a, mod4(b - step), every), t, k, 14 + step, along(axis, -step))
            left, right = sides(k)
            plane = out_at(t, k, a, every, every)
            ship(plane, plane, t, k, 18, right)
            ship(plane, plane, t, k, 19, left)

    def relay_send(t):
        for k in range(3):
            a = first_axis(k)
            left, right = sides(k)
            here(out_at(t, k, mod4(a - 1), every, every), t, k, 18, left)
            part = out_at(t, k, mod4(a - 1), lower, every)
            ship(part, part, t, k, 20, right)
            here(out_at(t, k, mod4(a + 1), every, every), t, k, 19, right)
            part = out_at(t, k, mod4(a + 1), upper, every)
            ship(part, part, t, k, 21, left)

    def finish(t):
        for k in range(3):
            a, b, c = (pos[axis] for axis in ORDER[k])
            left, right = sides(k)
            here(out_at(t, k, mod4(a + 2), lower, every), t, k, 20, left)
            here(out_at(t, k, mod4(a + 2), upper, every), t, k, 21, right)
            g = grad[t][k]

            def sent(src, i, t=t, k=k):
                wait_send(src, sems(t, k, i), partner)

            sent(g.at[2, lower], 0)
            sent(g.at[2, upper], 1)
            sent(g.at[1, upper], 2)
            sent(g.at[3, lower], 3)
            sent(g.at[1, lower], 4)
            sent(g.at[3, upper], 5)
            for step in range(1, 4):
                sent(s1[t][k].at[mod4(pos[ORDER[k][1]] + step)], 5 + step)
                sent(s2[t][k].at[mod4(pos[ORDER[k][2]] + step)], 8 + step)
                sent(out_at(t, k, a, b, c), 11 + step)
                sent(out_at(t, k, a, b, every), 14 + step)
            sent(out_at(t, k, a, every, every), 18)
            sent(out_at(t, k, a, every, every), 19)
            sent(out_at(t, k, mod4(a - 1), lower, every), 20)
            sent(out_at(t, k, mod4(a + 1), upper, every), 21)

    def make_up():
        def body(j, carry):
            for k in range(3):
                a = mod4(first_axis(k) + j)
                cols = pl.ds(pl.multiple_of(a * ACOL + UP_OFF[k], 128), UP_W[k])
                g = jnp.dot(act_t[...], cv[:, cols], preferred_element_type=F32)
                grad[0][k][j] = g.astype(BF).reshape(4, 4, 16, UP_W[k])
            return carry

        lax.fori_loop(0, RING, body, 0)
        stage1_send(0)

    def make_down(d_hidden):
        def body(j, carry):
            for k in range(3):
                a = mod4(first_axis(k) + j)
                h = DN_H[k]
                lhs = nt[a, :, DN_OFF[k]:DN_OFF[k] + h, :].reshape(16 * h, ROWS)
                g = jnp.dot(lhs, d_hidden, preferred_element_type=F32)
                grad[1][k][j] = g.astype(BF).reshape(4, 4, h, R)
            return carry

        lax.fori_loop(0, RING, body, 0)
        stage1_send(1)

    def hidden_grad(d_active):
        return (d_active * gate * (1.0 + hidden * (1.0 - gate))).astype(BF)

    def row_pass(d_hidden, send):
        mean = jnp.sum(d_hidden.astype(F32) * hidden, axis=1, keepdims=True) / D

        def body(c, carry):
            cols = cols_of(c)
            d_normed = lax.dot_general(d_hidden, wd_v[cols, :], INNER, preferred_element_type=F32)
            x_hat = x_v[:, cols].astype(F32) * inv
            gg[0, :, cols] = jnp.sum(d_normed * x_hat, axis=0, keepdims=True)
            d_in = cv[:, cols].astype(F32) + inv * (d_normed * gain_ref[:, cols] - x_hat * mean)
            out_rows[:, cols] = d_in.astype(BF)
            if send:
                rcopy(
                    out_rows.at[:, cols], cv.at[:, cols], row_ssem.at[c], row_rsem.at[c], partner
                ).start()
            return carry

        lax.fori_loop(0, N_CH, body, 0)

    @pl.when(sec == 1)
    def _():
        make_up()

        def body(c, acc):
            return acc + lax.dot_general(
                cv[:, cols_of(c)], wu_v[:, cols_of(c)], INNER, preferred_element_type=F32
            )

        d_hidden = hidden_grad(lax.fori_loop(0, N_CH, body, jnp.zeros((ROWS, R), F32)))
        row_pass(d_hidden, True)
        make_down(d_hidden)

    @pl.when(sec == 0)
    def _():
        def body(c, acc):
            row_wait(cv, c).wait_recv()
            return acc + lax.dot_general(
                cv[:, cols_of(c)], wu_v[:, cols_of(c)], INNER, preferred_element_type=F32
            )

        d_active = lax.fori_loop(0, N_CH, body, jnp.zeros((ROWS, R), F32))
        make_up()
        d_hidden = hidden_grad(d_active)
        make_down(d_hidden)
        row_pass(d_hidden, False)

    def gain_send(stage):
        axis = 2 - stage
        for step in range(1, 4):
            rcopy(
                gg.at[stage], gin.at[stage, step - 1],
                gain_ssem.at[stage, step - 1], gain_rsem.at[stage, step - 1], along(axis, step),
            ).start()

    def gain_add(stage):
        axis = 2 - stage
        for step in range(1, 4):
            wait_recv(
                gin.at[stage, step - 1],
                (gain_ssem.at[stage, step - 1], gain_rsem.at[stage, step - 1]), along(axis, -step),
            )
        gg[stage + 1] = gg[stage] + gin[stage, 0] + gin[stage, 1] + gin[stage, 2]

    gain_send(0)
    both = (0, 1)
    for t in both:
        stage1_merge(t)
    gain_add(0)
    gain_send(1)
    for t in both:
        stage2_send(t)
    gain_add(1)
    gain_send(2)
    for t in both:
        stage3_send(t)
    gain_add(2)
    out_gain[...] = (gg[3] * FACTOR).astype(BF)
    for t in both:
        gather1_send(t)
    for t in both:
        gather2_send(t)
    for t in both:
        gather3_send(t)
    for t in both:
        relay_send(t)
    for t in both:
        finish(t)

    for stage in range(3):
        for step in range(1, 4):
            wait_send(
                gg.at[stage], (gain_ssem.at[stage, step - 1], gain_rsem.at[stage, step - 1]), partner
            )

    @pl.when(sec == 0)
    def _():
        rcopy(a2a_send, a2a_send, a2a_ssem, a2a_rsem.at[0], partner).wait_send()

        def sent(c, carry):
            row_wait(fo, c).wait_send()
            return carry

        lax.fori_loop(0, N_CH, sent, 0)

    @pl.when(sec == 1)
    def _():
        rest = a2a_send.at[pl.ds(0, N_PEER - 1)]
        rcopy(rest, rest, a2a_ssem, a2a_rsem.at[1], partner).wait_send()

        def sent(c, carry):
            row_wait(out_rows, c).wait_send()
            return carry

        lax.fori_loop(0, N_CH, sent, 0)


def both_kinds(lead):
    ups = [pltpu.VMEM((*lead, 16, w), BF) for w in UP_W]
    downs = [pltpu.VMEM((*lead, h, R), BF) for h in DN_H]
    return ups + downs


def write_out(*refs):
    n = (len(refs) - 1) // 2
    sem = refs[-1]
    copies = [pltpu.make_async_copy(refs[i], refs[n + i], sem.at[i]) for i in range(n)]
    for copy in copies:
        copy.start()
    for copy in copies:
        copy.wait()


def shards(inputs, routes, counts, cotangent, gain_vector, w_down, w_up):
    hbm = pl.BlockSpec(memory_space=pl.ANY)
    vmem = pl.BlockSpec(memory_space=pltpu.VMEM)
    dma = pltpu.SemaphoreType.DMA
    scratch = [
        pltpu.VMEM((ROWS, D), BF),
        pltpu.VMEM((D, R), BF),
        pltpu.VMEM((R, D), BF),
        pltpu.VMEM((SLOTS, HALF), BF),
        pltpu.VMEM((N_PEER, 16, QUART), BF),
        pltpu.VMEM((2, N_PEER, 16, QUART), BF),
        pltpu.VMEM((RING, 16, 80, ROWS), BF),
        pltpu.VMEM((ROWS, D), BF),
        pltpu.VMEM((ROWS, D), BF),
        pltpu.VMEM((4 * ROWS, N_PEER * 16), BF),
        pltpu.VMEM((R, ROWS), BF),
    ]
    for lead in ((4, 4, 4), (2, 2, 4), (2, 4, 4), (4, 4), (3, 4), (4,), (3,)):
        scratch += both_kinds(lead)
    scratch += [
        pltpu.VMEM((4, 1, D), F32),
        pltpu.VMEM((3, 3, 1, D), F32),
        dma((4,)),
        dma,
        dma,
        dma((2,)),
        dma((N_CH,)),
        dma((N_CH,)),
        dma((2, 3, 22)),
        dma((2, 3, 22)),
        dma((3, 3)),
        dma((3, 3)),
    ]
    shapes = [(1, D), (RING, RING, RING, 80, R), (RING, RING, 16, D), (ROWS, D)]
    made = pl.pallas_call(
        kernel,
        out_shape=[pltpu.VMEM(s, BF) for s in shapes],
        in_specs=[hbm, vmem, vmem, hbm, vmem, hbm, hbm],
        out_specs=[vmem] * 4,
        scratch_shapes=scratch,
        compiler_params=pltpu.CompilerParams(
            collective_id=0, has_side_effects=True, vmem_limit_bytes=44 * 2**20
        ),
    )(inputs, routes, counts.reshape(1, 1), cotangent, gain_vector, w_down, w_up)
    gain, down, up, rows = pl.pallas_call(
        write_out,
        out_shape=[jax.ShapeDtypeStruct(s, BF) for s in shapes],
        in_specs=[vmem] * 4,
        out_specs=[hbm] * 4,
        scratch_shapes=[dma((4,))],
    )(*made)
    return gain, down.reshape(1, D, R), up.reshape(1, R, D), rows[None]


def solution(mesh):
    in_specs = (
        P("peer", None),
        P("peer", None),
        P("peer"),
        P("peer", None, None),
        P("section", None),
        P("section", None, None),
        P("section", None, None),
    )
    out_specs = (
        P("section", None),
        P("section", None, None),
        P("section", None, None),
        P("section", "peer", None),
    )
    return jax.shard_map(shards, mesh=mesh, in_specs=in_specs, out_specs=out_specs, check_vma=False)
```

time: 641 us -> 105 us (0.16)
  blocking collectives: 350 us -> 0 us
  waiting for transfers between devices: 126 us -> 0 us
  Pallas kernels: 0 us -> 95.7 us
  starting transfers between devices: 47.8 us -> 0 us
  other arithmetic: 41.1 us -> 0 us
  local copies, waits for them, and re-layouts: 42.2 us -> 7.52 us
  matrix products: 18.2 us -> 0 us
  between operations: 14.8 us -> 1.3 us
    psum x1 -> x0, blocking collectives: 350 us -> none  [shards(): summed = lax.psum((own_grads[0], own_grads[1], own_grads[2]), 'peer')]
    all_to_all x2 -> x0, waiting for transfers between devices: 126 us -> none  [the longest x1 63 us: shards(): lax.all_to_all(padded, ('section', 'peer'), split_axis=0, concat_axis=0,...]
    pallas_call x0 -> x2, Pallas kernels: none -> 95.7 us  [the longest x1 90 us: shards(): pl.pallas_call(kernel, out_shape=[pltpu.VMEM(s, BF) for s in shapes], in_...]
    all_to_all x2 -> x0, starting transfers between devices: 47.8 us -> none  [the longest x1 36.2 us: shards(): lax.all_to_all(doubled, ('section', 'peer'), split_axis=0, concat_axis=0,...]
    dot_general x6 -> x0, matrix products: 18.2 us -> none  [the longest x1 4.47 us: layer_backward(): lax.dot_general(normed, d_hidden, outer, preferred_element_type=jnp.float32)]
    add x3 -> x0, other arithmetic: 14.2 us -> none  [shards(): own_grads = jax.tree.map(lambda a, b: a + b, grads_first, grads_second)]
    gather x3 -> x0, local copies, waits for them, and re-layouts: 10.2 us -> none  [the longest x2 7.81 us: shards(): jnp.take(first_out, source_row, axis=0, mode='fill', fill_value=0)]
    reshape x2 -> x0, local copies, waits for them, and re-layouts: 8.28 us -> none  [the longest x1 4.25 us: shards(): back_slots = back_slots.reshape(n_peer, capacity, feature_dim)]
  transfers between devices with their start and end apart: 3 -> 0, of which waited for: 2 -> 0; matrix products, arithmetic and copies ran while one was open for 0% -> 0% of each run, Pallas kernels for 0% -> 0%
where the time goes in v1:
time: 105 us; the launch traced here: 104 us
  Pallas kernels  95.7 us (91%)
  local copies, waits for them, and re-layouts  7.52 us (7%)
  between operations  1.3 us (1%)
    pallas_call x1, Pallas kernels, shards(): pl.pallas_call(kernel, out_shape=[pltpu.VMEM(s, BF) for s in shapes], in_...  90 us
    unnamed x13, local copies, waits for them, and re-layouts  7.52 us
    pallas_call x1, Pallas kernels, shards(): pl.pallas_call(write_out, out_shape=[jax.ShapeDtypeStruct(s, BF) for s in...  5.72 us

profile of v1, /device:TPU:0, one launch (start us, length us, event | category | flops | bytes accessed | tf_op | source)
XLA Modules:
  0.0 104.5 jit_solution(14342263658247662273)
XLA Ops:
  1.3 0.8 copy.11.routes_ref
  2.0 0.0 copy-start.3
  2.0 1.3 %copy-done.3 = bf16[128,5120]{1,0:T(8,128)(2,1)S(1)} copy-done((bf16[128,5120]{1,0:T(8,128)(2,1)S(1)}, bf16[128,5120]{1,0:T(8,128)(2,1)}, u32[]{:S(2)}) %copy-start.3) | copy-done | bytes 1310744
  3.4 0.0 copy-start.4
  3.4 0.7 copy-done.4
  4.1 90.0 %shard_map.102 = (bf16[1,5120]{1,0:T(2,128)(2,1)S(1)}, bf16[4,4,4,80,256]{4,3,2,1,0:T(8,128)(2,1)S(1)}, bf16[4,4,16,5120]{3,2,1,0:T(8,128)(2,1)S(1)}, bf16[128,5120]{1,0:T(8,128)(2,1)S(1)}) custom-call(bf16[128,5120]{1,0:T(8,128)(2,1)S(1)} %copy-done.3, s32[128,1]{1,0:T(8,128)S(1)} %copy.11.routes_ref, s32[1,1]{1,0:T(1,128)} %bitcast.4.counts_ref, ...), custom_call_target="tpu_custom_call" | custom-call | tf_op jit(solution)/shard_map/pallas_call | solution.py:576
  94.0 0.0 copy-start
  94.1 1.5 %copy-done = bf16[4,4,4,80,256]{4,3,2,1,0:T(8,128)(2,1)} copy-done((bf16[4,4,4,80,256]{4,3,2,1,0:T(8,128)(2,1)}, bf16[4,4,4,80,256]{4,3,2,1,0:T(8,128)(2,1)S(1)}, u32[]{:S(2)}) %copy-start) | copy-done | bytes 2621464
  95.6 0.0 copy-start.1
  95.6 1.5 %copy-done.1 = bf16[4,4,16,5120]{3,2,1,0:T(8,128)(2,1)} copy-done((bf16[4,4,16,5120]{3,2,1,0:T(8,128)(2,1)}, bf16[4,4,16,5120]{3,2,1,0:T(8,128)(2,1)S(1)}, u32[]{:S(2)}) %copy-start.1) | copy-done | bytes 2621464
  97.1 0.0 copy-start.2
  97.1 1.1 %copy-done.2 = bf16[128,5120]{1,0:T(8,128)(2,1)} copy-done((bf16[128,5120]{1,0:T(8,128)(2,1)}, bf16[128,5120]{1,0:T(8,128)(2,1)S(1)}, u32[]{:S(2)}) %copy-start.2) | copy-done | bytes 1310744
  98.2 0.0 copy-start.5
  98.2 0.6 copy-done.5
  98.8 5.7 %shard_map.103 = (bf16[1,5120]{1,0:T(2,128)(2,1)}, bf16[4,4,4,80,256]{4,3,2,1,0:T(8,128)(2,1)}, bf16[4,4,16,5120]{3,2,1,0:T(8,128)(2,1)}, bf16[128,5120]{1,0:T(8,128)(2,1)}) custom-call(bf16[1,5120]{1,0:T(2,128)(2,1)} %copy-done.5, bf16[4,4,4,80,256]{4,3,2,1,0:T(8,128)(2,1)} %copy-done, bf16[4,4,16,5120]{3,2,1,0:T(8,128)(2,1)} %copy-done.1, ...), custom_call_target="tpu_custom_call" | custom-call | tf_op jit(solution)/shard_map/pallas_call | solution.py:586
Async XLA Ops:
  2.0 1.3 %copy-start.3 = (bf16[128,5120]{1,0:T(8,128)(2,1)S(1)}, bf16[128,5120]{1,0:T(8,128)(2,1)}, u32[]{:S(2)}) copy-start(bf16[128,5120]{1,0:T(8,128)(2,1)} %x_hbm.1) | copy-start | bytes 3932164
  3.4 0.7 copy-start.4
  94.0 1.5 %copy-start = (bf16[4,4,4,80,256]{4,3,2,1,0:T(8,128)(2,1)}, bf16[4,4,4,80,256]{4,3,2,1,0:T(8,128)(2,1)S(1)}, u32[]{:S(2)}) copy-start(bf16[4,4,4,80,256]{4,3,2,1,0:T(8,128)(2,1)S(1)} %get-tuple-element.13.refs_1_) | copy-start | bytes 7864324
  95.6 1.5 %copy-start.1 = (bf16[4,4,16,5120]{3,2,1,0:T(8,128)(2,1)}, bf16[4,4,16,5120]{3,2,1,0:T(8,128)(2,1)S(1)}, u32[]{:S(2)}) copy-start(bf16[4,4,16,5120]{3,2,1,0:T(8,128)(2,1)S(1)} %get-tuple-element.14.refs_2_) | copy-start | bytes 7864324
  97.1 1.1 %copy-start.2 = (bf16[128,5120]{1,0:T(8,128)(2,1)}, bf16[128,5120]{1,0:T(8,128)(2,1)S(1)}, u32[]{:S(2)}) copy-start(bf16[128,5120]{1,0:T(8,128)(2,1)S(1)} %get-tuple-element.15.refs_3_) | copy-start | bytes 3932164
  98.2 0.6 copy-start.5

commit v2 on v1

--- a/solution.py
+++ b/solution.py
@@ -15,6 +15,9 @@
 N_PEER, RING = 64, 4
 HALF = D // 2
 QUART = HALF // 4
+STRIDE, UNSTRIDE = 21, 3
+GROUP = 16
+N_GROUP = N_PEER // GROUP
 CH = 640
 N_CH = D // CH
 ACOL = D // RING
@@ -49,9 +52,9 @@
 
 
 def kernel(
-    x_hbm, routes_ref, counts_ref, cot_hbm, gain_ref, wd_hbm, wu_hbm,
+    x_hbm, routes_ref, counts_ref, cot_hbm, gain_hbm, wd_hbm, wu_hbm,
     out_gain, out_dn, out_up, out_rows,
-    x_v, wd_v, wu_v, cot_v, a2a_send, a2a_recv, nt, cv, fo, sel, act_t,
+    x_v, gain_ref, wd_v, wu_v, cot_v, a2a_send, a2a_recv, early_send, early_recv, nt, cv, fo, rest, sel, act_t,
     gu0, gu1, gu2, gd0, gd1, gd2,
     ru0, ru1, ru2, rd0, rd1, rd2,
     iu0, iu1, iu2, id0, id1, id2,
@@ -60,7 +63,7 @@
     s2u0, s2u1, s2u2, s2d0, s2d1, s2d2,
     i3u0, i3u1, i3u2, i3d0, i3d1, i3d2,
     gg, gin,
-    load_sem, own_sem, a2a_ssem, a2a_rsem, row_ssem, row_rsem, red_ssem, red_rsem, gain_ssem, gain_rsem,
+    load_sem, own_sem, a2a_ssem, a2a_rsem, early_ssem, early_rsem, row_ssem, row_rsem, red_ssem, red_rsem, gain_ssem, gain_rsem,
 ):
     grad = ((gu0, gu1, gu2), (gd0, gd1, gd2))
     rly = ((ru0, ru1, ru2), (rd0, rd1, rd2))
@@ -81,20 +84,27 @@
 
     partner = (1 - sec, me)
 
-    cot_load = pltpu.make_async_copy(
-        cot_hbm.at[0, :, pl.ds(pl.multiple_of(sec * HALF, HALF), HALF)], cot_v, load_sem.at[0]
-    )
-    wd_load = pltpu.make_async_copy(wd_hbm.at[0], wd_v, load_sem.at[1])
-    wu_load = pltpu.make_async_copy(wu_hbm.at[0], wu_v, load_sem.at[2])
-    x_load = pltpu.make_async_copy(x_hbm, x_v, load_sem.at[3])
-    cot_load.start()
+    def half_load(h):
+        cols = pl.ds(h * HALF, HALF)
+        return pltpu.make_async_copy(cot_hbm.at[0, :, cols], cot_v.at[:, cols], load_sem.at[h])
+
+    wd_load = pltpu.make_async_copy(wd_hbm.at[0], wd_v, load_sem.at[2])
+    wu_load = pltpu.make_async_copy(wu_hbm.at[0], wu_v, load_sem.at[3])
+    x_load = pltpu.make_async_copy(x_hbm, x_v, load_sem.at[4])
+    gain_load = pltpu.make_async_copy(gain_hbm, gain_ref, load_sem.at[5])
+    half_load(0).start()
 
     @pl.when(sec == 0)
     def _():
         x_load.start()
 
+    @pl.when(sec == 1)
+    def _():
+        half_load(1).start()
+
+    wu_load.start()
     wd_load.start()
-    wu_load.start()
+    gain_load.start()
 
     barrier = pltpu.get_barrier_semaphore()
 
@@ -115,52 +125,75 @@
 
         lax.fori_loop(1, N_PEER, greet, 0)
 
-    cot_load.wait()
+    def cols_of(c):
+        return pl.ds(pl.multiple_of(c * CH, CH), CH)
+
+    half_load(0).wait()
     o_i = lax.broadcasted_iota(jnp.int32, (SLOTS, SLOTS), 0)
     i_i = lax.broadcasted_iota(jnp.int32, (SLOTS, SLOTS), 1)
     perm = jnp.where(i_i == (o_i & 3) * 64 + (o_i >> 2), 1.0, 0.0).astype(BF)
 
+    def blocks(quarters, width):
+        moved = jnp.dot(perm, jnp.concatenate(quarters, axis=0), preferred_element_type=F32)
+        return moved.astype(BF).reshape(16, 16, width)
+
     def arrange(g, carry):
         rows = pl.ds(pl.multiple_of(g * 64, 64), 64)
-        block = jnp.concatenate(
-            [cot_v[rows, j * QUART:(j + 1) * QUART] for j in range(4)], axis=0
+        a2a_send[pl.ds(pl.multiple_of(g * 16, 16), 16)] = blocks(
+            [cot_v[rows, pl.ds(pl.multiple_of(sec * HALF + j * QUART, 128), QUART)] for j in range(4)], QUART
         )
-        moved = jnp.dot(perm, block, preferred_element_type=F32).astype(BF)
-        a2a_send[pl.ds(pl.multiple_of(g * 16, 16), 16)] = moved.reshape(16, 16, QUART)
         return carry
 
-    lax.fori_loop(0, 4, arrange, 0)
+    def peer_at(i):
+        return lax.rem(me + i * STRIDE, N_PEER)
+
+    def send_rows(h):
+        def send(i, carry):
+            dst = peer_at(i)
+            rcopy(
+                a2a_send.at[dst], a2a_recv.at[h, i], a2a_ssem, a2a_rsem.at[h, i // GROUP], (1, dst)
+            ).start()
+            return carry
+
+        lax.fori_loop(h, N_PEER, send, 0)
 
     @pl.when(sec == 0)
     def _():
+        lax.fori_loop(0, 4, arrange, 0)
         pl.semaphore_wait(barrier, 10)
-
-        def send(i, carry):
-            dst = lax.rem(me + i * 21, N_PEER)
-            rcopy(
-                a2a_send.at[dst], a2a_recv.at[0, me], a2a_ssem, a2a_rsem.at[0], (1, dst)
-            ).start()
-            return carry
-
-        lax.fori_loop(0, N_PEER, send, 0)
+        send_rows(0)
 
     @pl.when(sec == 1)
     def _():
+        half_load(1).wait()
+        wu_load.wait()
+
+        def body(c, acc):
+            return acc + lax.dot_general(
+                cot_v[:, cols_of(c)], wu_v[:, cols_of(c)], INNER, preferred_element_type=F32
+            )
+
+        d_slot = lax.fori_loop(0, N_CH, body, jnp.zeros((SLOTS, R), F32))
+        high = d_slot.astype(BF)
+        low = (d_slot - high.astype(F32)).astype(BF)
+        for g in range(4):
+            rows = slice(g * 64, (g + 1) * 64)
+            early_send[g * 16:(g + 1) * 16] = blocks(
+                [part[rows, lo:lo + 128] for part in (high, low) for lo in (0, 128)], 128
+            )
         pl.semaphore_wait(barrier, N_PEER)
         pl.semaphore_signal(barrier, inc=1, device_id=partner, device_id_type=MESH)
-        pltpu.make_async_copy(a2a_send.at[me], a2a_recv.at[1, me], own_sem).start()
+        pltpu.make_async_copy(early_send.at[me], early_recv.at[0], own_sem.at[0]).start()
 
         def send(i, carry):
-            dst = lax.rem(me + i * 21, N_PEER)
-            rcopy(
-                a2a_send.at[dst], a2a_recv.at[1, me], a2a_ssem, a2a_rsem.at[1], (1, dst)
-            ).start()
+            dst = peer_at(i)
+            rcopy(early_send.at[dst], early_recv.at[i], early_ssem, early_rsem, (1, dst)).start()
             return carry
 
         lax.fori_loop(1, N_PEER, send, 0)
-
-    def cols_of(c):
-        return pl.ds(pl.multiple_of(c * CH, CH), CH)
+        lax.fori_loop(0, 4, arrange, 0)
+        pltpu.make_async_copy(a2a_send.at[me], a2a_recv.at[1, 0], own_sem.at[1]).start()
+        send_rows(1)
 
     def row_wait(ref, c):
         return rcopy(ref.at[:, cols_of(c)], ref.at[:, cols_of(c)], row_ssem.at[c], row_rsem.at[c], partner)
@@ -179,6 +212,7 @@
 
     total = lax.fori_loop(0, N_CH, squares, jnp.zeros((ROWS, 1), F32))
     inv = lax.rsqrt(total / D + rms_eps)
+    gain_load.wait()
     wd_load.wait()
 
     def down(c, hidden):
@@ -191,10 +225,10 @@
     gate = jax.nn.sigmoid(hidden)
     active = (hidden * gate).astype(BF)
     act_t[...] = active.T
-    wu_load.wait()
-
     @pl.when(sec == 0)
     def _():
+        wu_load.wait()
+
         def up(c, carry):
             y = jnp.dot(active, wu_v[:, cols_of(c)], preferred_element_type=F32)
             fo[:, cols_of(c)] = (x_v[:, cols_of(c)].astype(F32) + y).astype(BF)
@@ -205,33 +239,56 @@
 
         lax.fori_loop(0, N_CH, up, 0)
 
-    @pl.when(sec == 1)
-    def _():
+    def choose():
         dest = routes_ref[...]
-        live = lax.broadcasted_iota(jnp.int32, (ROWS, 1), 0) < counts_ref[...]
+        live = lax.broadcasted_iota(jnp.int32, (1, ROWS), 1) < counts_ref[...]
         lane = lax.broadcasted_iota(jnp.int32, (ROWS, ROWS), 1)
         row = lax.broadcasted_iota(jnp.int32, (ROWS, ROWS), 0)
-        named = jnp.where((lane == dest) & live, 1.0, 0.0)
-        before = jnp.where(lane < row, 1.0, 0.0).astype(BF)
-        rank = jnp.dot(before, named.astype(BF), preferred_element_type=F32)
-        nth = jnp.sum(named * rank, axis=1, keepdims=True)
-        place = jnp.where(live, dest.astype(F32) * 16.0 + nth * 4.0, -16.0)
+        named = jnp.where((row == dest) & live, 1.0, 0.0)
+        before = jnp.where(row < lane, 1.0, 0.0).astype(BF)
+        rank = jnp.dot(named.astype(BF), before, preferred_element_type=F32)
+        nth = jnp.sum(named * rank, axis=0, keepdims=True)
+        turn = ((dest + (N_PEER - me)) * UNSTRIDE) & (N_PEER - 1)
+        across = jnp.where(live, turn.astype(F32) * 16.0 + nth * 4.0, -16.0)
+        place = jnp.sum(jnp.where(row == lane, across, 0.0), axis=1, keepdims=True)
         column = lax.broadcasted_iota(jnp.int32, (ROWS, N_PEER * 16), 1).astype(F32)
         for j in range(4):
             sel[j * ROWS:(j + 1) * ROWS, :] = jnp.where(column == place + float(j), 1.0, 0.0).astype(BF)
+
+    def early_active():
+        pltpu.make_async_copy(early_send.at[me], early_recv.at[0], own_sem.at[0]).wait()
+        others = early_recv.at[pl.ds(1, N_PEER - 1)]
+        rcopy(others, others, early_ssem, early_rsem, partner).wait_recv()
+        got = jnp.dot(
+            sel[...], early_recv[...].reshape(N_PEER * 16, 128), preferred_element_type=F32
+        ).reshape(4, ROWS, 128)
+        return jnp.concatenate([got[0] + got[2], got[1] + got[3]], axis=1)
+
+    def pick(g):
+        group = pl.ds(g * GROUP, GROUP)
         for h in range(2):
-            if h == 0:
-                rcopy(a2a_recv.at[0], a2a_recv.at[0], a2a_ssem, a2a_rsem.at[0], partner).wait_recv()
-            else:
-                pltpu.make_async_copy(a2a_send.at[me], a2a_recv.at[1, me], own_sem).wait()
-                rest = a2a_recv.at[1, pl.ds(0, N_PEER - 1)]
-                rcopy(rest, rest, a2a_ssem, a2a_rsem.at[1], partner).wait_recv()
-            for n in range(QUART // 128):
-                block = a2a_recv[h, :, :, n * 128:(n + 1) * 128].reshape(N_PEER * 16, 128)
-                picked = jnp.dot(sel[...], block, preferred_element_type=F32).astype(BF)
-                for j in range(4):
-                    lo = h * HALF + j * QUART + n * 128
-                    cv[:, lo:lo + 128] = picked[j * ROWS:(j + 1) * ROWS, :]
+            landed = a2a_recv.at[h, group]
+            if h == 1 and g == 0:
+                pltpu.make_async_copy(a2a_send.at[me], a2a_recv.at[1, 0], own_sem.at[1]).wait()
+                landed = a2a_recv.at[1, pl.ds(1, GROUP - 1)]
+            rcopy(landed, landed, a2a_ssem, a2a_rsem.at[h, g], partner).wait_recv()
+            picked = jnp.dot(
+                sel[:, g * GROUP * 16:(g + 1) * GROUP * 16],
+                a2a_recv[h, group].reshape(GROUP * 16, QUART),
+                preferred_element_type=F32,
+            ).astype(BF)
+            for j in range(4):
+                cols = pl.ds((h * 4 + j) * CH, CH)
+                part = picked[j * ROWS:(j + 1) * ROWS, :]
+                if g > 0:
+                    part = cv[:, cols] + part
+                cv[:, cols] = part
+                if g == N_GROUP - 1:
+                    out_rows[:, cols] = (part.astype(F32) + rest[:, cols]).astype(BF)
+                    rcopy(
+                        out_rows.at[:, cols], cv.at[:, cols],
+                        row_ssem.at[h * 4 + j], row_rsem.at[h * 4 + j], partner,
+                    ).start()
 
     def out_at(t, k, a, b, c):
         if t == 0:
@@ -338,27 +395,31 @@
             for step in range(1, 4):
                 here(out_at(t, k, a, mod4(b - step), every), t, k, 14 + step, along(axis, -step))
             left, right = sides(k)
-            plane = out_at(t, k, a, every, every)
-            ship(plane, plane, t, k, 18, right)
-            ship(plane, plane, t, k, 19, left)
+            low, high = out_at(t, k, a, lower, every), out_at(t, k, a, upper, every)
+            ship(low, low, t, k, 18, right)
+            ship(high, high, t, k, 19, left)
+            ship(high, high, t, k, 20, right)
+            ship(low, low, t, k, 21, left)
 
     def relay_send(t):
         for k in range(3):
             a = first_axis(k)
             left, right = sides(k)
-            here(out_at(t, k, mod4(a - 1), every, every), t, k, 18, left)
             part = out_at(t, k, mod4(a - 1), lower, every)
-            ship(part, part, t, k, 20, right)
-            here(out_at(t, k, mod4(a + 1), every, every), t, k, 19, right)
+            here(part, t, k, 18, left)
+            ship(part, part, t, k, 22, right)
             part = out_at(t, k, mod4(a + 1), upper, every)
-            ship(part, part, t, k, 21, left)
+            here(part, t, k, 19, right)
+            ship(part, part, t, k, 23, left)
 
     def finish(t):
         for k in range(3):
             a, b, c = (pos[axis] for axis in ORDER[k])
             left, right = sides(k)
-            here(out_at(t, k, mod4(a + 2), lower, every), t, k, 20, left)
-            here(out_at(t, k, mod4(a + 2), upper, every), t, k, 21, right)
+            here(out_at(t, k, mod4(a - 1), upper, every), t, k, 20, left)
+            here(out_at(t, k, mod4(a + 1), lower, every), t, k, 21, right)
+            here(out_at(t, k, mod4(a + 2), lower, every), t, k, 22, left)
+            here(out_at(t, k, mod4(a + 2), upper, every), t, k, 23, right)
             g = grad[t][k]
 
             def sent(src, i, t=t, k=k):
@@ -375,10 +436,12 @@
                 sent(s2[t][k].at[mod4(pos[ORDER[k][2]] + step)], 8 + step)
                 sent(out_at(t, k, a, b, c), 11 + step)
                 sent(out_at(t, k, a, b, every), 14 + step)
-            sent(out_at(t, k, a, every, every), 18)
-            sent(out_at(t, k, a, every, every), 19)
-            sent(out_at(t, k, mod4(a - 1), lower, every), 20)
-            sent(out_at(t, k, mod4(a + 1), upper, every), 21)
+            sent(out_at(t, k, a, lower, every), 18)
+            sent(out_at(t, k, a, upper, every), 19)
+            sent(out_at(t, k, a, upper, every), 20)
+            sent(out_at(t, k, a, lower, every), 21)
+            sent(out_at(t, k, mod4(a - 1), lower, every), 22)
+            sent(out_at(t, k, mod4(a + 1), upper, every), 23)
 
     def make_up():
         def body(j, carry):
@@ -408,7 +471,7 @@
     def hidden_grad(d_active):
         return (d_active * gate * (1.0 + hidden * (1.0 - gate))).astype(BF)
 
-    def row_pass(d_hidden, send):
+    def row_pass(d_hidden, last):
         mean = jnp.sum(d_hidden.astype(F32) * hidden, axis=1, keepdims=True) / D
 
         def body(c, carry):
@@ -416,28 +479,26 @@
             d_normed = lax.dot_general(d_hidden, wd_v[cols, :], INNER, preferred_element_type=F32)
             x_hat = x_v[:, cols].astype(F32) * inv
             gg[0, :, cols] = jnp.sum(d_normed * x_hat, axis=0, keepdims=True)
-            d_in = cv[:, cols].astype(F32) + inv * (d_normed * gain_ref[:, cols] - x_hat * mean)
-            out_rows[:, cols] = d_in.astype(BF)
-            if send:
-                rcopy(
-                    out_rows.at[:, cols], cv.at[:, cols], row_ssem.at[c], row_rsem.at[c], partner
-                ).start()
+            change = inv * (d_normed * gain_ref[:, cols] - x_hat * mean)
+            if last:
+                out_rows[:, cols] = (cv[:, cols].astype(F32) + change).astype(BF)
+            else:
+                rest[:, cols] = change
             return carry
 
         lax.fori_loop(0, N_CH, body, 0)
 
     @pl.when(sec == 1)
     def _():
+        choose()
+        pick(0)
+        d_hidden = hidden_grad(early_active())
+        make_down(d_hidden)
+        pick(1)
+        row_pass(d_hidden, False)
+        pick(2)
+        pick(3)
         make_up()
-
-        def body(c, acc):
-            return acc + lax.dot_general(
-                cv[:, cols_of(c)], wu_v[:, cols_of(c)], INNER, preferred_element_type=F32
-            )
-
-        d_hidden = hidden_grad(lax.fori_loop(0, N_CH, body, jnp.zeros((ROWS, R), F32)))
-        row_pass(d_hidden, True)
-        make_down(d_hidden)
 
     @pl.when(sec == 0)
     def _():
@@ -447,11 +508,10 @@
                 cv[:, cols_of(c)], wu_v[:, cols_of(c)], INNER, preferred_element_type=F32
             )
 
-        d_active = lax.fori_loop(0, N_CH, body, jnp.zeros((ROWS, R), F32))
+        d_hidden = hidden_grad(lax.fori_loop(0, N_CH, body, jnp.zeros((ROWS, R), F32)))
+        make_down(d_hidden)
         make_up()
-        d_hidden = hidden_grad(d_active)
-        make_down(d_hidden)
-        row_pass(d_hidden, False)
+        row_pass(d_hidden, True)
 
     def gain_send(stage):
         axis = 2 - stage
@@ -471,7 +531,7 @@
         gg[stage + 1] = gg[stage] + gin[stage, 0] + gin[stage, 1] + gin[stage, 2]
 
     gain_send(0)
-    both = (0, 1)
+    both = (1, 0)
     for t in both:
         stage1_merge(t)
     gain_add(0)
@@ -503,7 +563,7 @@
 
     @pl.when(sec == 0)
     def _():
-        rcopy(a2a_send, a2a_send, a2a_ssem, a2a_rsem.at[0], partner).wait_send()
+        rcopy(a2a_send, a2a_send, a2a_ssem, early_rsem, partner).wait_send()
 
         def sent(c, carry):
             row_wait(fo, c).wait_send()
@@ -513,8 +573,9 @@
 
     @pl.when(sec == 1)
     def _():
-        rest = a2a_send.at[pl.ds(0, N_PEER - 1)]
-        rcopy(rest, rest, a2a_ssem, a2a_rsem.at[1], partner).wait_send()
+        for sent_from, sem in ((a2a_send, a2a_ssem), (early_send, early_ssem)):
+            others = sent_from.at[pl.ds(0, N_PEER - 1)]
+            rcopy(others, others, sem, early_rsem, partner).wait_send()
 
         def sent(c, carry):
             row_wait(out_rows, c).wait_send()
@@ -539,20 +600,28 @@
         copy.wait()
 
 
+def stay(operand):
+    return pltpu.with_memory_space_constraint(operand, pltpu.HBM)
+
+
 def shards(inputs, routes, counts, cotangent, gain_vector, w_down, w_up):
-    hbm = pl.BlockSpec(memory_space=pl.ANY)
+    hbm = pl.BlockSpec(memory_space=pltpu.HBM)
     vmem = pl.BlockSpec(memory_space=pltpu.VMEM)
     dma = pltpu.SemaphoreType.DMA
     scratch = [
         pltpu.VMEM((ROWS, D), BF),
+        pltpu.VMEM((1, D), F32),
         pltpu.VMEM((D, R), BF),
         pltpu.VMEM((R, D), BF),
-        pltpu.VMEM((SLOTS, HALF), BF),
+        pltpu.VMEM((SLOTS, D), BF),
         pltpu.VMEM((N_PEER, 16, QUART), BF),
         pltpu.VMEM((2, N_PEER, 16, QUART), BF),
+        pltpu.VMEM((N_PEER, 16, 128), BF),
+        pltpu.VMEM((N_PEER, 16, 128), BF),
         pltpu.VMEM((RING, 16, 80, ROWS), BF),
         pltpu.VMEM((ROWS, D), BF),
         pltpu.VMEM((ROWS, D), BF),
+        pltpu.VMEM((ROWS, D), F32),
         pltpu.VMEM((4 * ROWS, N_PEER * 16), BF),
         pltpu.VMEM((R, ROWS), BF),
     ]
@@ -561,14 +630,16 @@
     scratch += [
         pltpu.VMEM((4, 1, D), F32),
         pltpu.VMEM((3, 3, 1, D), F32),
-        dma((4,)),
+        dma((6,)),
+        dma((2,)),
+        dma,
+        dma((2, N_GROUP)),
         dma,
         dma,
-        dma((2,)),
         dma((N_CH,)),
         dma((N_CH,)),
-        dma((2, 3, 22)),
-        dma((2, 3, 22)),
+        dma((2, 3, 24)),
+        dma((2, 3, 24)),
         dma((3, 3)),
         dma((3, 3)),
     ]
@@ -582,13 +653,17 @@
         compiler_params=pltpu.CompilerParams(
             collective_id=0, has_side_effects=True, vmem_limit_bytes=44 * 2**20
         ),
-    )(inputs, routes, counts.reshape(1, 1), cotangent, gain_vector, w_down, w_up)
+    )(
+        stay(inputs), routes.reshape(1, ROWS), counts.reshape(1, 1), stay(cotangent), stay(gain_vector),
+        stay(w_down), stay(w_up),
+    )
     gain, down, up, rows = pl.pallas_call(
         write_out,
         out_shape=[jax.ShapeDtypeStruct(s, BF) for s in shapes],
         in_specs=[vmem] * 4,
         out_specs=[hbm] * 4,
         scratch_shapes=[dma((4,))],
+        compiler_params=pltpu.CompilerParams(vmem_limit_bytes=2**20),
     )(*made)
     return gain, down.reshape(1, D, R), up.reshape(1, R, D), rows[None]
 

time: 105 us -> 90.7 us (0.86)
  Pallas kernels: 95.7 us -> 88.6 us
  local copies, waits for them, and re-layouts: 7.52 us -> 0.65 us
    unnamed x13 -> x2, local copies, waits for them, and re-layouts: 7.52 us -> 0.65 us
    pallas_call x1, Pallas kernels: 90 us -> 85.8 us  [shards(): pl.pallas_call(kernel, out_shape=[pltpu.VMEM(s, BF) for s in shapes], in_...]
    pallas_call x1, Pallas kernels: 5.72 us -> 2.83 us  [shards(): pl.pallas_call(write_out, out_shape=[jax.ShapeDtypeStruct(s, BF) for s in...]
where the time goes in v2:
time: 90.7 us; the launch traced here: 90.6 us
  Pallas kernels  88.6 us (98%)
  between operations  1.29 us (1%)
    pallas_call x1, Pallas kernels, shards(): pl.pallas_call(kernel, out_shape=[pltpu.VMEM(s, BF) for s in shapes], in_...  85.8 us
    pallas_call x1, Pallas kernels, shards(): pl.pallas_call(write_out, out_shape=[jax.ShapeDtypeStruct(s, BF) for s in...  2.83 us

profile of v2, /device:TPU:0, one launch (start us, length us, event | category | flops | bytes accessed | tf_op | source)
XLA Modules:
  0.0 90.6 jit_solution(1365287141619018229)
XLA Ops:
  1.3 0.0 copy-start
  1.3 0.6 copy-done
  1.9 85.8 %shard_map.102 = (bf16[1,5120]{1,0:T(2,128)(2,1)S(1)}, bf16[4,4,4,80,256]{4,3,2,1,0:T(8,128)(2,1)S(1)}, bf16[4,4,16,5120]{3,2,1,0:T(8,128)(2,1)S(1)}, bf16[128,5120]{1,0:T(8,128)(2,1)S(1)}) custom-call(bf16[128,5120]{1,0:T(8,128)(2,1)} %x_hbm.1, s32[1,128]{1,0:T(1,128)S(1)} %bitcast.6, s32[1,1]{1,0:T(1,128)} %bitcast.5.counts_ref, ...), custom_call_target="tpu_custom_call" | custom-call | tf_op jit(solution)/shard_map/pallas_call | solution.py:647
  87.7 2.8 %shard_map.103 = (bf16[1,5120]{1,0:T(2,128)(2,1)}, bf16[4,4,4,80,256]{4,3,2,1,0:T(8,128)(2,1)}, bf16[4,4,16,5120]{3,2,1,0:T(8,128)(2,1)}, bf16[128,5120]{1,0:T(8,128)(2,1)}) custom-call(bf16[1,5120]{1,0:T(2,128)(2,1)S(1)} %get-tuple-element.12.refs_0_, bf16[4,4,4,80,256]{4,3,2,1,0:T(8,128)(2,1)S(1)} %get-tuple-element.13.refs_1_, ...), custom_call_target="tpu_custom_call" | custom-call | tf_op jit(solution)/shard_map/pallas_call | solution.py:660
Async XLA Ops:
  1.3 0.7 copy-start

commit v3 on v2

v3 whole, which is shorter than its diff:
```python
import jax
import jax.numpy as jnp
from jax import lax
from jax.experimental import pallas as pl
from jax.experimental.pallas import tpu as pltpu
from jax.sharding import PartitionSpec as P

rms_eps = 1e-05
MESH = pl.DeviceIdType.MESH
BF = jnp.bfloat16
F32 = jnp.float32

ROWS, D, R = 128, 5120, 256
SLOTS, CAP = 256, 4
N_PEER, RING = 64, 4
HALF = D // 2
QUART = HALF // 4
GROUP = 16
N_GROUP = N_PEER // GROUP
UNROLL = 4
CH = 640
N_CH = D // CH
ACOL = D // RING
UP_OFF, UP_W = (0, 384, 768), (384, 384, 512)
DN_OFF, DN_H = (0, 32, 64), (32, 32, 16)
ORDER = ((0, 1, 2), (1, 2, 0), (2, 0, 1))
FACTOR = float(N_PEER * ROWS) ** (-0.5)
INNER = (((1,), (1,)), ((), ()))


def mod4(v):
    return lax.rem(v + 8, 4)


def rcopy(src, dst, send_sem, recv_sem, device):
    return pltpu.make_async_remote_copy(
        src_ref=src,
        dst_ref=dst,
        send_sem=send_sem,
        recv_sem=recv_sem,
        device_id=device,
        device_id_type=MESH,
    )


def wait_recv(dst, sems, device):
    rcopy(dst, dst, sems[0], sems[1], device).wait_recv()


def wait_send(src, sems, device):
    rcopy(src, src, sems[0], sems[1], device).wait_send()


def kernel(
    x_hbm, routes_hbm, counts_hbm, cot_hbm, gain_hbm, wd_hbm, wu_hbm,
    out_gain, out_dn, out_up, out_rows,
    x_v, routes_ref, counts_ref, gain_ref, wd_v, wu_v, cot_v, a2a_send, a2a_recv, early_send, early_recv, nt, cv, fo, rest, sel, act_t,
    gu0, gu1, gu2, gd0, gd1, gd2,
    ru0, ru1, ru2, rd0, rd1, rd2,
    iu0, iu1, iu2, id0, id1, id2,
    su0, su1, su2, sd0, sd1, sd2,
    i2u0, i2u1, i2u2, i2d0, i2d1, i2d2,
    i3u0, i3u1, i3u2, i3d0, i3d1, i3d2,
    gg, gin,
    load_sem, own_sem, a2a_ssem, a2a_rsem, early_ssem, early_rsem, row_ssem, row_rsem, red_ssem, red_rsem, gain_ssem, gain_rsem,
):
    grad = ((gu0, gu1, gu2), (gd0, gd1, gd2))
    rly = ((ru0, ru1, ru2), (rd0, rd1, rd2))
    inb = ((iu0, iu1, iu2), (id0, id1, id2))
    s1 = ((su0, su1, su2), (sd0, sd1, sd2))
    in2 = ((i2u0, i2u1, i2u2), (i2d0, i2d1, i2d2))
    in3 = ((i3u0, i3u1, i3u2), (i3d0, i3d1, i3d2))

    sec = lax.axis_index("section")
    me = lax.axis_index("peer")
    pos = (me // 16, lax.rem(me // 4, 4), lax.rem(me, 4))
    weight = (16, 4, 1)

    def along(axis, step):
        there = mod4(pos[axis] + step)
        return (sec, me + (there - pos[axis]) * weight[axis])

    partner = (1 - sec, me)

    def half_load(h):
        cols = pl.ds(h * HALF, HALF)
        return pltpu.make_async_copy(cot_hbm.at[0, :, cols], cot_v.at[:, cols], load_sem.at[h])

    wd_load = pltpu.make_async_copy(wd_hbm.at[0], wd_v, load_sem.at[2])
    wu_load = pltpu.make_async_copy(wu_hbm.at[0], wu_v, load_sem.at[3])
    x_load = pltpu.make_async_copy(x_hbm, x_v, load_sem.at[4])
    gain_load = pltpu.make_async_copy(gain_hbm, gain_ref, load_sem.at[5])
    routes_load = pltpu.make_async_copy(routes_hbm, routes_ref, load_sem.at[6])
    counts_load = pltpu.make_async_copy(counts_hbm, counts_ref, load_sem.at[7])
    barrier = pltpu.get_barrier_semaphore()

    def cols_of(c):
        return pl.ds(pl.multiple_of(c * CH, CH), CH)

    def blocks(quarters, width):
        o_i = lax.broadcasted_iota(jnp.int32, (SLOTS, SLOTS), 0)
        i_i = lax.broadcasted_iota(jnp.int32, (SLOTS, SLOTS), 1)
        perm = jnp.where(i_i == (o_i & 3) * 64 + (o_i >> 2), 1.0, 0.0).astype(BF)
        moved = jnp.dot(perm, jnp.concatenate(quarters, axis=0), preferred_element_type=F32)
        return moved.astype(BF).reshape(16, 16, width)

    def arrange(h):
        for g in range(4):
            rows = slice(g * 64, (g + 1) * 64)
            starts = [h * HALF + j * QUART for j in range(4)]
            a2a_send[g * 16:(g + 1) * 16] = blocks([cot_v[rows, lo:lo + QUART] for lo in starts], QUART)

    def peer_at(i):
        i2, i1, i0 = i // 16, lax.rem(i // 4, 4), lax.rem(i, 4)
        return mod4(pos[0] + i2 + i0) * 16 + mod4(pos[1] + i1 + i0) * 4 + mod4(pos[2] + i0)

    def send_rows(h):
        def send(i, carry):
            dst = peer_at(i)
            rcopy(
                a2a_send.at[dst], a2a_recv.at[h, i], a2a_ssem, a2a_rsem.at[h, i // GROUP], (1, dst)
            ).start()
            return carry

        lax.fori_loop(h, N_PEER, send, 0)

    def arrange_early():
        def body(c, acc):
            return acc + lax.dot_general(
                cot_v[:, cols_of(c)], wu_v[:, cols_of(c)], INNER, preferred_element_type=F32
            )

        d_slot = lax.fori_loop(0, N_CH, body, jnp.zeros((SLOTS, R), F32), unroll=UNROLL)
        high = d_slot.astype(BF)
        low = (d_slot - high.astype(F32)).astype(BF)
        for g in range(4):
            rows = slice(g * 64, (g + 1) * 64)
            early_send[g * 16:(g + 1) * 16] = blocks(
                [part[rows, lo:lo + 128] for part in (high, low) for lo in (0, 128)], 128
            )

    def send_early():
        pltpu.make_async_copy(early_send.at[me], early_recv.at[0], own_sem.at[0]).start()

        def send(i, carry):
            dst = peer_at(i)
            rcopy(early_send.at[dst], early_recv.at[i], early_ssem, early_rsem, (1, dst)).start()
            return carry

        lax.fori_loop(1, N_PEER, send, 0)

    def row_wait(ref, c):
        return rcopy(ref.at[:, cols_of(c)], ref.at[:, cols_of(c)], row_ssem.at[c], row_rsem.at[c], partner)

    def scaled(c):
        return (x_v[:, cols_of(c)].astype(F32) * gain_ref[:, cols_of(c)]).astype(BF)

    def turn_rows(c, carry):
        half = pl.ds(pl.multiple_of(lax.rem(c, 2) * 8, 8), 8)
        nt[c // 2, half] = scaled(c).T.reshape(8, 80, ROWS)
        return carry

    def forward(arriving):
        def down(c, carry):
            raw, total = carry
            if arriving:
                row_wait(x_v, c).wait_recv()
            xf = x_v[:, cols_of(c)].astype(F32)
            total = total + jnp.sum(xf * xf, axis=1, keepdims=True)
            return raw + jnp.dot(scaled(c), wd_v[cols_of(c), :], preferred_element_type=F32), total

        start = jnp.zeros((ROWS, R), F32), jnp.zeros((ROWS, 1), F32)
        raw, total = lax.fori_loop(0, N_CH, down, start, unroll=UNROLL)
        inv = lax.rsqrt(total / D + rms_eps)
        hidden = raw * inv
        gate = jax.nn.sigmoid(hidden)
        active = (hidden * gate).astype(BF)
        act_t[...] = active.T
        return inv, hidden, gate, active

    def choose():
        dest = routes_ref[...]
        live = lax.broadcasted_iota(jnp.int32, (1, ROWS), 1) < counts_ref[...]
        lane = lax.broadcasted_iota(jnp.int32, (ROWS, ROWS), 1)
        row = lax.broadcasted_iota(jnp.int32, (ROWS, ROWS), 0)
        named = jnp.where((row == dest) & live, 1.0, 0.0)
        before = jnp.where(row < lane, 1.0, 0.0).astype(BF)
        rank = jnp.dot(named.astype(BF), before, preferred_element_type=F32)
        nth = jnp.sum(named * rank, axis=0, keepdims=True)
        z = (pos[2] + 4 - (dest & 3)) & 3
        x = (pos[1] + 8 - ((dest >> 2) & 3) - z) & 3
        y = (pos[0] + 8 - (dest >> 4) - z) & 3
        turn = y * 16 + x * 4 + z
        across = jnp.where(live, turn.astype(F32) * 16.0 + nth * 4.0, -16.0)
        place = jnp.sum(jnp.where(row == lane, across, 0.0), axis=1, keepdims=True)
        column = lax.broadcasted_iota(jnp.int32, (ROWS, N_PEER * 16), 1).astype(F32)
        for j in range(4):
            sel[j * ROWS:(j + 1) * ROWS, :] = jnp.where(column == place + float(j), 1.0, 0.0).astype(BF)

    def early_active():
        pltpu.make_async_copy(early_send.at[me], early_recv.at[0], own_sem.at[0]).wait()
        others = early_recv.at[pl.ds(1, N_PEER - 1)]
        rcopy(others, others, early_ssem, early_rsem, partner).wait_recv()
        got = jnp.dot(
            sel[...], early_recv[...].reshape(N_PEER * 16, 128), preferred_element_type=F32
        ).reshape(4, ROWS, 128)
        return jnp.concatenate([got[0] + got[2], got[1] + got[3]], axis=1)

    def pick(g):
        group = pl.ds(g * GROUP, GROUP)
        for h in range(2):
            landed = a2a_recv.at[h, group]
            if h == 1 and g == 0:
                pltpu.make_async_copy(a2a_send.at[me], a2a_recv.at[1, 0], own_sem.at[1]).wait()
                landed = a2a_recv.at[1, pl.ds(1, GROUP - 1)]
            rcopy(landed, landed, a2a_ssem, a2a_rsem.at[h, g], partner).wait_recv()
            picked = jnp.dot(
                sel[:, g * GROUP * 16:(g + 1) * GROUP * 16],
                a2a_recv[h, group].reshape(GROUP * 16, QUART),
                preferred_element_type=F32,
            ).astype(BF)
            for j in range(4):
                cols = pl.ds((h * 4 + j) * CH, CH)
                part = picked[j * ROWS:(j + 1) * ROWS, :]
                if g > 0:
                    part = cv[:, cols] + part
                cv[:, cols] = part
                if g == N_GROUP - 1:
                    out_rows[:, cols] = (part.astype(F32) + rest[:, cols]).astype(BF)
                    rcopy(
                        out_rows.at[:, cols], cv.at[:, cols],
                        row_ssem.at[h * 4 + j], row_rsem.at[h * 4 + j], partner,
                    ).start()

    def out_at(t, k, a, b, c):
        if t == 0:
            cols = pl.ds(pl.multiple_of(a * ACOL + UP_OFF[k], 128), UP_W[k])
            return out_up.at[b, c, :, cols]
        return out_dn.at[a, b, c, pl.ds(DN_OFF[k], DN_H[k]), :]

    every = pl.ds(0, RING)
    lower, upper = pl.ds(0, 2), pl.ds(2, 2)

    def sems(t, k, i):
        return red_ssem.at[t, k], red_rsem.at[t, k, i]

    def ship(src, dst, t, k, i, device):
        rcopy(src, dst, *sems(t, k, i), device).start()

    def here(dst, t, k, i):
        wait_recv(dst, sems(t, k, i), partner)

    def first_axis(k):
        return pos[ORDER[k][0]]

    def sides(k):
        axis = ORDER[k][0]
        return along(axis, -1), along(axis, 1)

    def stage1_send(t):
        for k in range(3):
            g, left, right = grad[t][k], *sides(k)
            ship(g.at[2, lower], rly[t][k].at[0], t, k, 0, right)
            ship(g.at[2, upper], rly[t][k].at[1], t, k, 1, left)
            ship(g.at[1, upper], inb[t][k].at[0, upper], t, k, 2, right)
            ship(g.at[3, lower], inb[t][k].at[1, lower], t, k, 2, left)

    def stage1_merge(t):
        for k in range(3):
            g, left, right = grad[t][k], *sides(k)
            here(rly[t][k].at[0], t, k, 0)
            g[1, 0:2] = (g[1, 0:2].astype(F32) + rly[t][k][0].astype(F32)).astype(BF)
            ship(g.at[1, lower], inb[t][k].at[0, lower], t, k, 2, right)
            here(rly[t][k].at[1], t, k, 1)
            g[3, 2:4] = (g[3, 2:4].astype(F32) + rly[t][k][1].astype(F32)).astype(BF)
            ship(g.at[3, upper], inb[t][k].at[1, upper], t, k, 2, left)

    def stage2_send(t):
        for k in range(3):
            g, box, part = grad[t][k], inb[t][k], s1[t][k]
            here(box, t, k, 2)

            def add(b, carry, g=g, box=box, part=part):
                part[b] = (g[0, b].astype(F32) + box[0, b].astype(F32) + box[1, b].astype(F32)).astype(BF)
                return carry

            lax.fori_loop(0, RING, add, 0)
            axis = ORDER[k][1]
            for step in range(1, 4):
                ship(part.at[mod4(pos[axis] + step)], in2[t][k].at[step - 1], t, k, 3, along(axis, step))

    def stage3_send(t):
        for k in range(3):
            box, line = in2[t][k], in3[t][k]
            here(box, t, k, 3)
            mine = s1[t][k][pos[ORDER[k][1]]].astype(F32)
            axis = ORDER[k][2]
            part = line.at[pos[axis]]
            part[...] = (mine + box[0].astype(F32) + box[1].astype(F32) + box[2].astype(F32)).astype(BF)
            for step in range(1, 4):
                ship(part, part, t, k, 4, along(axis, step))

    def gather2_send(t):
        for k in range(3):
            a, b, _ = (pos[axis] for axis in ORDER[k])
            box = in3[t][k]
            here(box.at[0:3], t, k, 4)
            whole = box[0].astype(F32) + box[1].astype(F32) + box[2].astype(F32) + box[3].astype(F32)
            mine = out_at(t, k, a, b, every)
            mine[...] = (whole * FACTOR).astype(BF)
            axis = ORDER[k][1]
            for step in range(1, 4):
                ship(mine, mine, t, k, 6, along(axis, step))

    def gather3_send(t):
        for k in range(3):
            here(in2[t][k], t, k, 6)
            left, right = sides(k)
            a = first_axis(k)
            low, high = out_at(t, k, a, lower, every), out_at(t, k, a, upper, every)
            ship(low, low, t, k, 7, right)
            ship(high, high, t, k, 8, left)
            ship(high, high, t, k, 9, right)
            ship(low, low, t, k, 9, left)

    def relay_send(t):
        for k in range(3):
            a = first_axis(k)
            left, right = sides(k)
            part = out_at(t, k, mod4(a - 1), lower, every)
            here(part, t, k, 7)
            ship(part, part, t, k, 9, right)
            part = out_at(t, k, mod4(a + 1), upper, every)
            here(part, t, k, 8)
            ship(part, part, t, k, 9, left)

    def finish(t):
        for k in range(3):
            here(inb[t][k], t, k, 9)
            g = grad[t][k]
            for sent in (g, g, g.at[0, 0]):
                wait_send(sent, sems(t, k, 0), partner)

    def make_up():
        def body(j, carry):
            for k in range(3):
                a = mod4(first_axis(k) + j)
                cols = pl.ds(pl.multiple_of(a * ACOL + UP_OFF[k], 128), UP_W[k])
                g = jnp.dot(act_t[...], cv[:, cols], preferred_element_type=F32)
                grad[0][k][j] = g.astype(BF).reshape(4, 4, 16, UP_W[k])
            return carry

        lax.fori_loop(0, RING, body, 0)
        stage1_send(0)

    def make_down(d_hidden, inv):
        d_scaled = (d_hidden * inv).astype(BF)

        def body(j, carry):
            for k in range(3):
                a = mod4(first_axis(k) + j)
                h = DN_H[k]
                lhs = nt[a, :, DN_OFF[k]:DN_OFF[k] + h, :].reshape(16 * h, ROWS)
                g = jnp.dot(lhs, d_scaled, preferred_element_type=F32)
                grad[1][k][j] = g.astype(BF).reshape(4, 4, h, R)
            return carry

        lax.fori_loop(0, RING, body, 0)
        stage1_send(1)

    def hidden_grad(d_active, hidden, gate):
        return d_active * gate * (1.0 + hidden * (1.0 - gate))

    def row_pass(d_hidden, hidden, inv, last):
        d_hidden = d_hidden.astype(BF)
        mean = jnp.sum(d_hidden.astype(F32) * hidden, axis=1, keepdims=True) / D

        def body(c, carry):
            cols = cols_of(c)
            d_normed = lax.dot_general(d_hidden, wd_v[cols, :], INNER, preferred_element_type=F32)
            x_hat = x_v[:, cols].astype(F32) * inv
            gg[0, :, cols] = jnp.sum(d_normed * x_hat, axis=0, keepdims=True)
            change = inv * (d_normed * gain_ref[:, cols] - x_hat * mean)
            if last:
                out_rows[:, cols] = (cv[:, cols].astype(F32) + change).astype(BF)
            else:
                rest[:, cols] = change
            return carry

        lax.fori_loop(0, N_CH, body, 0, unroll=UNROLL)

    @pl.when(sec == 1)
    def _():
        half_load(1).start()
        half_load(0).start()
        wu_load.start()

        def greet(i, carry):
            pl.semaphore_signal(barrier, inc=1, device_id=(0, peer_at(i)), device_id_type=MESH)
            return carry

        lax.fori_loop(0, N_PEER, greet, 0)
        routes_load.start()
        counts_load.start()
        gain_load.start()
        wd_load.start()
        half_load(1).wait()
        arrange(1)
        half_load(0).wait()
        wu_load.wait()
        arrange_early()
        pl.semaphore_wait(barrier, 1)
        send_early()
        pltpu.make_async_copy(a2a_send.at[me], a2a_recv.at[1, 0], own_sem.at[1]).start()
        send_rows(1)
        routes_load.wait()
        counts_load.wait()
        choose()
        gain_load.wait()
        wd_load.wait()
        inv, hidden, gate, _ = forward(True)
        pick(0)
        lax.fori_loop(0, N_CH, turn_rows, 0, unroll=UNROLL)
        d_hidden = hidden_grad(early_active(), hidden, gate)
        make_down(d_hidden, inv)
        pick(1)
        row_pass(d_hidden, hidden, inv, False)
        pick(2)
        pick(3)
        make_up()

    @pl.when(sec == 0)
    def _():
        half_load(0).start()
        x_load.start()
        gain_load.start()
        wd_load.start()
        wu_load.start()
        for axis in range(3):
            for step in range(1, 4):
                pl.semaphore_signal(barrier, inc=1, device_id=along(axis, step), device_id_type=MESH)
        half_load(0).wait()
        arrange(0)
        pl.semaphore_wait(barrier, N_PEER + 9)
        pl.semaphore_signal(barrier, inc=1, device_id=partner, device_id_type=MESH)
        send_rows(0)
        x_load.wait()
        gain_load.wait()
        wd_load.wait()
        inv, hidden, gate, active = forward(False)
        wu_load.wait()

        def up(c, carry):
            y = jnp.dot(active, wu_v[:, cols_of(c)], preferred_element_type=F32)
            fo[:, cols_of(c)] = (x_v[:, cols_of(c)].astype(F32) + y).astype(BF)
            rcopy(
                fo.at[:, cols_of(c)], x_v.at[:, cols_of(c)], row_ssem.at[c], row_rsem.at[c], partner
            ).start()
            return carry

        lax.fori_loop(0, N_CH, up, 0, unroll=UNROLL)
        lax.fori_loop(0, N_CH, turn_rows, 0, unroll=UNROLL)

        def body(c, acc):
            row_wait(cv, c).wait_recv()
            return acc + lax.dot_general(
                cv[:, cols_of(c)], wu_v[:, cols_of(c)], INNER, preferred_element_type=F32
            )

        d_active = lax.fori_loop(0, N_CH, body, jnp.zeros((ROWS, R), F32), unroll=UNROLL)
        d_hidden = hidden_grad(d_active, hidden, gate)
        make_down(d_hidden, inv)
        make_up()
        row_pass(d_hidden, hidden, inv, True)

    def gain_send(stage):
        axis = 2 - stage
        for step in range(1, 4):
            rcopy(
                gg.at[stage], gin.at[stage, step - 1], gain_ssem, gain_rsem.at[stage], along(axis, step)
            ).start()

    def gain_add(stage):
        wait_recv(gin.at[stage], (gain_ssem, gain_rsem.at[stage]), partner)
        gg[stage + 1] = gg[stage] + gin[stage, 0] + gin[stage, 1] + gin[stage, 2]

    gain_send(0)
    both = (1, 0)
    for t in both:
        stage1_merge(t)
    gain_add(0)
    gain_send(1)
    for t in both:
        stage2_send(t)
    gain_add(1)
    gain_send(2)
    for t in both:
        stage3_send(t)
    gain_add(2)
    out_gain[...] = (gg[3] * FACTOR).astype(BF)
    for t in both:
        gather2_send(t)
    for t in both:
        gather3_send(t)
    for t in both:
        relay_send(t)
    for t in both:
        finish(t)

    wait_send(gin, (gain_ssem, gain_rsem.at[0]), partner)

    @pl.when(sec == 0)
    def _():
        rcopy(a2a_send, a2a_send, a2a_ssem, early_rsem, partner).wait_send()

        def sent(c, carry):
            row_wait(fo, c).wait_send()
            return carry

        lax.fori_loop(0, N_CH, sent, 0)

    @pl.when(sec == 1)
    def _():
        for sent_from, sem in ((a2a_send, a2a_ssem), (early_send, early_ssem)):
            others = sent_from.at[pl.ds(0, N_PEER - 1)]
            rcopy(others, others, sem, early_rsem, partner).wait_send()

        def sent(c, carry):
            row_wait(out_rows, c).wait_send()
            return carry

        lax.fori_loop(0, N_CH, sent, 0)


def both_kinds(lead):
    ups = [pltpu.VMEM((*lead, 16, w), BF) for w in UP_W]
    downs = [pltpu.VMEM((*lead, h, R), BF) for h in DN_H]
    return ups + downs


def write_out(*refs):
    n = (len(refs) - 1) // 2
    sem = refs[-1]
    copies = [pltpu.make_async_copy(refs[i], refs[n + i], sem.at[i]) for i in range(n)]
    for copy in copies:
        copy.start()
    for copy in copies:
        copy.wait()


def stay(operand):
    return pltpu.with_memory_space_constraint(operand, pltpu.HBM)


def shards(inputs, routes, counts, cotangent, gain_vector, w_down, w_up):
    hbm = pl.BlockSpec(memory_space=pltpu.HBM)
    vmem = pl.BlockSpec(memory_space=pltpu.VMEM)
    anywhere = pl.BlockSpec(memory_space=pl.ANY)
    dma = pltpu.SemaphoreType.DMA
    scratch = [
        pltpu.VMEM((ROWS, D), BF),
        pltpu.VMEM((1, ROWS), jnp.int32),
        pltpu.VMEM((1, 1), jnp.int32),
        pltpu.VMEM((1, D), F32),
        pltpu.VMEM((D, R), BF),
        pltpu.VMEM((R, D), BF),
        pltpu.VMEM((SLOTS, D), BF),
        pltpu.VMEM((N_PEER, 16, QUART), BF),
        pltpu.VMEM((2, N_PEER, 16, QUART), BF),
        pltpu.VMEM((N_PEER, 16, 128), BF),
        pltpu.VMEM((N_PEER, 16, 128), BF),
        pltpu.VMEM((RING, 16, 80, ROWS), BF),
        pltpu.VMEM((ROWS, D), BF),
        pltpu.VMEM((ROWS, D), BF),
        pltpu.VMEM((ROWS, D), F32),
        pltpu.VMEM((4 * ROWS, N_PEER * 16), BF),
        pltpu.VMEM((R, ROWS), BF),
    ]
    for lead in ((4, 4, 4), (2, 2, 4), (2, 4, 4), (4, 4), (3, 4), (4, 4)):
        scratch += both_kinds(lead)
    scratch += [
        pltpu.VMEM((4, 1, D), F32),
        pltpu.VMEM((3, 3, 1, D), F32),
        dma((8,)),
        dma((2,)),
        dma,
        dma((2, N_GROUP)),
        dma,
        dma,
        dma((N_CH,)),
        dma((N_CH,)),
        dma((2, 3)),
        dma((2, 3, 10)),
        dma,
        dma((3,)),
    ]
    shapes = [(1, D), (RING, RING, RING, 80, R), (RING, RING, 16, D), (ROWS, D)]
    made = pl.pallas_call(
        kernel,
        out_shape=[pltpu.VMEM(s, BF) for s in shapes],
        in_specs=[hbm, anywhere, anywhere, hbm, hbm, hbm, hbm],
        out_specs=[vmem] * 4,
        scratch_shapes=scratch,
        compiler_params=pltpu.CompilerParams(
            collective_id=0, has_side_effects=True, vmem_limit_bytes=44 * 2**20
        ),
    )(
        stay(inputs), routes.reshape(1, ROWS), counts.reshape(1, 1), stay(cotangent), stay(gain_vector),
        stay(w_down), stay(w_up),
    )
    gain, down, up, rows = pl.pallas_call(
        write_out,
        out_shape=[jax.ShapeDtypeStruct(s, BF) for s in shapes],
        in_specs=[vmem] * 4,
        out_specs=[hbm] * 4,
        scratch_shapes=[dma((4,))],
        compiler_params=pltpu.CompilerParams(vmem_limit_bytes=2**20),
    )(*made)
    return gain, down.reshape(1, D, R), up.reshape(1, R, D), rows[None]


def solution(mesh):
    in_specs = (
        P("peer", None),
        P("peer", None),
        P("peer"),
        P("peer", None, None),
        P("section", None),
        P("section", None, None),
        P("section", None, None),
    )
    out_specs = (
        P("section", None),
        P("section", None, None),
        P("section", None, None),
        P("section", "peer", None),
    )
    return jax.shard_map(shards, mesh=mesh, in_specs=in_specs, out_specs=out_specs, check_vma=False)
```

time: 90.7 us -> 84.5 us (0.932)
  Pallas kernels: 88.6 us -> 82.5 us
    pallas_call x1, Pallas kernels: 85.8 us -> 79.6 us  [shards(): pl.pallas_call(kernel, out_shape=[pltpu.VMEM(s, BF) for s in shapes], in_...]
where the time goes in v3:
time: 84.5 us; the launch traced here: 84.4 us
  Pallas kernels  82.5 us (98%)
  between operations  1.29 us (2%)
    pallas_call x1, Pallas kernels, shards(): pl.pallas_call(kernel, out_shape=[pltpu.VMEM(s, BF) for s in shapes], in_...  79.6 us
    pallas_call x1, Pallas kernels, shards(): pl.pallas_call(write_out, out_shape=[jax.ShapeDtypeStruct(s, BF) for s in...  2.83 us

profile of v3, /device:TPU:0, one launch (start us, length us, event | category | flops | bytes accessed | tf_op | source)
XLA Modules:
  0.0 84.4 jit_solution(18358196079016045288)
XLA Ops:
  1.3 0.0 copy-start
  1.3 0.6 copy-done
  1.9 79.6 %shard_map.102 = (bf16[1,5120]{1,0:T(2,128)(2,1)S(1)}, bf16[4,4,4,80,256]{4,3,2,1,0:T(8,128)(2,1)S(1)}, bf16[4,4,16,5120]{3,2,1,0:T(8,128)(2,1)S(1)}, bf16[128,5120]{1,0:T(8,128)(2,1)S(1)}) custom-call(bf16[128,5120]{1,0:T(8,128)(2,1)} %x_hbm.1, s32[1,128]{1,0:T(1,128)S(1)} %bitcast.6, s32[1,1]{1,0:T(1,128)} %bitcast.5.counts_hbm, ...), custom_call_target="tpu_custom_call" | custom-call | tf_op jit(solution)/shard_map/pallas_call | solution.py:598
  81.6 2.8 %shard_map.103 = (bf16[1,5120]{1,0:T(2,128)(2,1)}, bf16[4,4,4,80,256]{4,3,2,1,0:T(8,128)(2,1)}, bf16[4,4,16,5120]{3,2,1,0:T(8,128)(2,1)}, bf16[128,5120]{1,0:T(8,128)(2,1)}) custom-call(bf16[1,5120]{1,0:T(2,128)(2,1)S(1)} %get-tuple-element.12.refs_0_, bf16[4,4,4,80,256]{4,3,2,1,0:T(8,128)(2,1)S(1)} %get-tuple-element.13.refs_1_, ...), custom_call_target="tpu_custom_call" | custom-call | tf_op jit(solution)/shard_map/pallas_call | solution.py:611
Async XLA Ops:
  1.3 0.7 copy-start

commit v4 on v3

--- a/solution.py
+++ b/solution.py
@@ -350,7 +350,7 @@
                 grad[0][k][j] = g.astype(BF).reshape(4, 4, 16, UP_W[k])
             return carry
 
-        lax.fori_loop(0, RING, body, 0)
+        lax.fori_loop(0, RING, body, 0, unroll=UNROLL)
         stage1_send(0)
 
     def make_down(d_hidden, inv):
@@ -365,7 +365,7 @@
                 grad[1][k][j] = g.astype(BF).reshape(4, 4, h, R)
             return carry
 
-        lax.fori_loop(0, RING, body, 0)
+        lax.fori_loop(0, RING, body, 0, unroll=UNROLL)
         stage1_send(1)
 
     def hidden_grad(d_active, hidden, gate):
@@ -605,7 +605,7 @@
             collective_id=0, has_side_effects=True, vmem_limit_bytes=44 * 2**20
         ),
     )(
-        stay(inputs), routes.reshape(1, ROWS), counts.reshape(1, 1), stay(cotangent), stay(gain_vector),
+        stay(inputs), stay(routes.reshape(1, ROWS)), counts.reshape(1, 1), stay(cotangent), stay(gain_vector),
         stay(w_down), stay(w_up),
     )
     gain, down, up, rows = pl.pallas_call(

time: 84.5 us -> 84 us (level)
  no operation moved by 1% of the time
where the time goes in v4:
time: 84 us; the launch traced here: 83.8 us
  Pallas kernels  82.4 us (98%)
  between operations  1.45 us (2%)
    pallas_call x1, Pallas kernels, shards(): pl.pallas_call(kernel, out_shape=[pltpu.VMEM(s, BF) for s in shapes], in_...  79.6 us
    pallas_call x1, Pallas kernels, shards(): pl.pallas_call(write_out, out_shape=[jax.ShapeDtypeStruct(s, BF) for s in...  2.83 us

profile of v4, /device:TPU:0, one launch (start us, length us, event | category | flops | bytes accessed | tf_op | source)
XLA Modules:
  0.0 83.8 jit_solution(3862905619573238233)
XLA Ops:
  1.3 79.6 %shard_map.102 = (bf16[1,5120]{1,0:T(2,128)(2,1)S(1)}, bf16[4,4,4,80,256]{4,3,2,1,0:T(8,128)(2,1)S(1)}, bf16[4,4,16,5120]{3,2,1,0:T(8,128)(2,1)S(1)}, bf16[128,5120]{1,0:T(8,128)(2,1)S(1)}) custom-call(bf16[128,5120]{1,0:T(8,128)(2,1)} %x_hbm.1, s32[1,128]{1,0:T(1,128)} %bitcast.6, s32[1,1]{1,0:T(1,128)} %bitcast.5.counts_hbm, ...), custom_call_target="tpu_custom_call" | custom-call | tf_op jit(solution)/shard_map/pallas_call | solution.py:598
  80.9 2.8 %shard_map.103 = (bf16[1,5120]{1,0:T(2,128)(2,1)}, bf16[4,4,4,80,256]{4,3,2,1,0:T(8,128)(2,1)}, bf16[4,4,16,5120]{3,2,1,0:T(8,128)(2,1)}, bf16[128,5120]{1,0:T(8,128)(2,1)}) custom-call(bf16[1,5120]{1,0:T(2,128)(2,1)S(1)} %get-tuple-element.12.refs_0_, bf16[4,4,4,80,256]{4,3,2,1,0:T(8,128)(2,1)S(1)} %get-tuple-element.13.refs_1_, ...), custom_call_target="tpu_custom_call" | custom-call | tf_op jit(solution)/shard_map/pallas_call | solution.py:611

commit v5 on v4

--- a/solution.py
+++ b/solution.py
@@ -60,6 +60,7 @@
     iu0, iu1, iu2, id0, id1, id2,
     su0, su1, su2, sd0, sd1, sd2,
     i2u0, i2u1, i2u2, i2d0, i2d1, i2d2,
+    s2u0, s2u1, s2u2, s2d0, s2d1, s2d2,
     i3u0, i3u1, i3u2, i3d0, i3d1, i3d2,
     gg, gin,
     load_sem, own_sem, a2a_ssem, a2a_rsem, early_ssem, early_rsem, row_ssem, row_rsem, red_ssem, red_rsem, gain_ssem, gain_rsem,
@@ -69,6 +70,7 @@
     inb = ((iu0, iu1, iu2), (id0, id1, id2))
     s1 = ((su0, su1, su2), (sd0, sd1, sd2))
     in2 = ((i2u0, i2u1, i2u2), (i2d0, i2d1, i2d2))
+    s2 = ((s2u0, s2u1, s2u2), (s2d0, s2d1, s2d2))
     in3 = ((i3u0, i3u1, i3u2), (i3d0, i3d1, i3d2))
 
     sec = lax.axis_index("section")
@@ -289,25 +291,61 @@
             for step in range(1, 4):
                 ship(part.at[mod4(pos[axis] + step)], in2[t][k].at[step - 1], t, k, 3, along(axis, step))
 
+    def line_sum(t, k):
+        box = in2[t][k]
+        here(box, t, k, 3)
+        mine = s1[t][k][pos[ORDER[k][1]]].astype(F32)
+        return (mine + box[0].astype(F32) + box[1].astype(F32) + box[2].astype(F32)).astype(BF)
+
     def stage3_send(t):
-        for k in range(3):
-            box, line = in2[t][k], in3[t][k]
-            here(box, t, k, 3)
-            mine = s1[t][k][pos[ORDER[k][1]]].astype(F32)
-            axis = ORDER[k][2]
-            part = line.at[pos[axis]]
-            part[...] = (mine + box[0].astype(F32) + box[1].astype(F32) + box[2].astype(F32)).astype(BF)
-            for step in range(1, 4):
-                ship(part, part, t, k, 4, along(axis, step))
+        @pl.when(sec == 0)
+        def _():
+            for k in range(3):
+                axis = ORDER[k][2]
+                part = in3[t][k].at[pos[axis]]
+                part[...] = line_sum(t, k)
+                for step in range(1, 4):
+                    ship(part, part, t, k, 4, along(axis, step))
+
+        @pl.when(sec == 1)
+        def _():
+            for k in range(3):
+                axis = ORDER[k][2]
+                part = s2[t][k]
+                part[...] = line_sum(t, k)
+                for step in range(1, 4):
+                    ship(part.at[mod4(pos[axis] + step)], in3[t][k].at[0, step - 1], t, k, 4, along(axis, step))
+
+    def gather1_send(t):
+        @pl.when(sec == 1)
+        def _():
+            for k in range(3):
+                a, b, c = (pos[axis] for axis in ORDER[k])
+                box = in3[t][k].at[0]
+                here(box.at[0:3], t, k, 4)
+                mine = s2[t][k][c].astype(F32)
+                whole = mine + box[0].astype(F32) + box[1].astype(F32) + box[2].astype(F32)
+                piece = out_at(t, k, a, b, c)
+                piece[...] = (whole * FACTOR).astype(BF)
+                for step in range(1, 4):
+                    ship(piece, piece, t, k, 5, along(ORDER[k][2], step))
 
     def gather2_send(t):
         for k in range(3):
             a, b, _ = (pos[axis] for axis in ORDER[k])
             box = in3[t][k]
-            here(box.at[0:3], t, k, 4)
-            whole = box[0].astype(F32) + box[1].astype(F32) + box[2].astype(F32) + box[3].astype(F32)
             mine = out_at(t, k, a, b, every)
-            mine[...] = (whole * FACTOR).astype(BF)
+
+            @pl.when(sec == 0)
+            def _(k=k, box=box, mine=mine):
+                here(box.at[0:3], t, k, 4)
+                whole = box[0].astype(F32) + box[1].astype(F32) + box[2].astype(F32) + box[3].astype(F32)
+                mine[...] = (whole * FACTOR).astype(BF)
+
+            @pl.when(sec == 1)
+            def _(k=k, box=box):
+                here(box.at[0, 0:3], t, k, 5)
+
             axis = ORDER[k][1]
             for step in range(1, 4):
                 ship(mine, mine, t, k, 6, along(axis, step))
@@ -338,8 +376,16 @@
         for k in range(3):
             here(inb[t][k], t, k, 9)
             g = grad[t][k]
-            for sent in (g, g, g.at[0, 0]):
-                wait_send(sent, sems(t, k, 0), partner)
+
+            @pl.when(sec == 0)
+            def _(k=k, g=g):
+                for sent in (g, g, g.at[0, 0]):
+                    wait_send(sent, sems(t, k, 0), partner)
+
+            @pl.when(sec == 1)
+            def _(k=k, g=g):
+                for sent in (g, g.at[0:3], g.at[3, 0:3], g.at[3, 3, 0:2]):
+                    wait_send(sent, sems(t, k, 0), partner)
 
     def make_up():
         def body(j, carry):
@@ -499,6 +545,8 @@
     gain_add(2)
     out_gain[...] = (gg[3] * FACTOR).astype(BF)
     for t in both:
+        gather1_send(t)
+    for t in both:
         gather2_send(t)
     for t in both:
         gather3_send(t)
@@ -576,7 +624,7 @@
         pltpu.VMEM((4 * ROWS, N_PEER * 16), BF),
         pltpu.VMEM((R, ROWS), BF),
     ]
-    for lead in ((4, 4, 4), (2, 2, 4), (2, 4, 4), (4, 4), (3, 4), (4, 4)):
+    for lead in ((4, 4, 4), (2, 2, 4), (2, 4, 4), (4, 4), (3, 4), (4,), (4, 4)):
         scratch += both_kinds(lead)
     scratch += [
         pltpu.VMEM((4, 1, D), F32),

time: 84 us -> 83.4 us (level)
  no operation moved by 1% of the time
where the time goes in v5:
time: 83.4 us; the launch traced here: 83.3 us
  Pallas kernels  81.8 us (98%)
  between operations  1.45 us (2%)
    pallas_call x1, Pallas kernels, shards(): pl.pallas_call(kernel, out_shape=[pltpu.VMEM(s, BF) for s in shapes], in_...  79 us
    pallas_call x1, Pallas kernels, shards(): pl.pallas_call(write_out, out_shape=[jax.ShapeDtypeStruct(s, BF) for s in...  2.83 us

profile of v5, /device:TPU:0, one launch (start us, length us, event | category | flops | bytes accessed | tf_op | source)
XLA Modules:
  0.0 83.3 jit_solution(3833578729668626257)
XLA Ops:
  1.3 79.0 %shard_map.102 = (bf16[1,5120]{1,0:T(2,128)(2,1)S(1)}, bf16[4,4,4,80,256]{4,3,2,1,0:T(8,128)(2,1)S(1)}, bf16[4,4,16,5120]{3,2,1,0:T(8,128)(2,1)S(1)}, bf16[128,5120]{1,0:T(8,128)(2,1)S(1)}) custom-call(bf16[128,5120]{1,0:T(8,128)(2,1)} %x_hbm.1, s32[1,128]{1,0:T(1,128)} %bitcast.6, s32[1,1]{1,0:T(1,128)} %bitcast.5.counts_hbm, ...), custom_call_target="tpu_custom_call" | custom-call | tf_op jit(solution)/shard_map/pallas_call | solution.py:646
  80.3 2.8 %shard_map.103 = (bf16[1,5120]{1,0:T(2,128)(2,1)}, bf16[4,4,4,80,256]{4,3,2,1,0:T(8,128)(2,1)}, bf16[4,4,16,5120]{3,2,1,0:T(8,128)(2,1)}, bf16[128,5120]{1,0:T(8,128)(2,1)}) custom-call(bf16[1,5120]{1,0:T(2,128)(2,1)S(1)} %get-tuple-element.12.refs_0_, bf16[4,4,4,80,256]{4,3,2,1,0:T(8,128)(2,1)S(1)} %get-tuple-element.13.refs_1_, ...), custom_call_target="tpu_custom_call" | custom-call | tf_op jit(solution)/shard_map/pallas_call | solution.py:659

commit v6 on v5

--- a/solution.py
+++ b/solution.py
@@ -465,10 +465,10 @@
         gain_load.wait()
         wd_load.wait()
         inv, hidden, gate, _ = forward(True)
-        pick(0)
         lax.fori_loop(0, N_CH, turn_rows, 0, unroll=UNROLL)
         d_hidden = hidden_grad(early_active(), hidden, gate)
         make_down(d_hidden, inv)
+        pick(0)
         pick(1)
         row_pass(d_hidden, hidden, inv, False)
         pick(2)
@@ -530,28 +530,28 @@
         wait_recv(gin.at[stage], (gain_ssem, gain_rsem.at[stage]), partner)
         gg[stage + 1] = gg[stage] + gin[stage, 0] + gin[stage, 1] + gin[stage, 2]
 
+    both = (1, 0)
+    for t in both:
+        stage1_merge(t)
+    for t in both:
+        stage2_send(t)
     gain_send(0)
-    both = (1, 0)
-    for t in both:
-        stage1_merge(t)
+    for t in both:
+        stage3_send(t)
     gain_add(0)
     gain_send(1)
     for t in both:
-        stage2_send(t)
+        gather1_send(t)
+    for t in both:
+        gather2_send(t)
     gain_add(1)
     gain_send(2)
     for t in both:
-        stage3_send(t)
+        gather3_send(t)
+    for t in both:
+        relay_send(t)
     gain_add(2)
     out_gain[...] = (gg[3] * FACTOR).astype(BF)
-    for t in both:
-        gather1_send(t)
-    for t in both:
-        gather2_send(t)
-    for t in both:
-        gather3_send(t)
-    for t in both:
-        relay_send(t)
     for t in both:
         finish(t)
 

time: 83.4 us -> 83.3 us (level)
  no operation moved by 1% of the time
where the time goes in v6:
time: 83.3 us; the launch traced here: 83.2 us
  Pallas kernels  81.8 us (98%)
  between operations  1.45 us (2%)
    pallas_call x1, Pallas kernels, shards(): pl.pallas_call(kernel, out_shape=[pltpu.VMEM(s, BF) for s in shapes], in_...  78.9 us
    pallas_call x1, Pallas kernels, shards(): pl.pallas_call(write_out, out_shape=[jax.ShapeDtypeStruct(s, BF) for s in...  2.83 us

profile of v6, /device:TPU:0, one launch (start us, length us, event | category | flops | bytes accessed | tf_op | source)
XLA Modules:
  0.0 83.2 jit_solution(6575870544026163301)
XLA Ops:
  1.3 78.9 %shard_map.102 = (bf16[1,5120]{1,0:T(2,128)(2,1)S(1)}, bf16[4,4,4,80,256]{4,3,2,1,0:T(8,128)(2,1)S(1)}, bf16[4,4,16,5120]{3,2,1,0:T(8,128)(2,1)S(1)}, bf16[128,5120]{1,0:T(8,128)(2,1)S(1)}) custom-call(bf16[128,5120]{1,0:T(8,128)(2,1)} %x_hbm.1, s32[1,128]{1,0:T(1,128)} %bitcast.6, s32[1,1]{1,0:T(1,128)} %bitcast.5.counts_hbm, ...), custom_call_target="tpu_custom_call" | custom-call | tf_op jit(solution)/shard_map/pallas_call | solution.py:646
  80.2 2.8 %shard_map.103 = (bf16[1,5120]{1,0:T(2,128)(2,1)}, bf16[4,4,4,80,256]{4,3,2,1,0:T(8,128)(2,1)}, bf16[4,4,16,5120]{3,2,1,0:T(8,128)(2,1)}, bf16[128,5120]{1,0:T(8,128)(2,1)}) custom-call(bf16[1,5120]{1,0:T(2,128)(2,1)S(1)} %get-tuple-element.12.refs_0_, bf16[4,4,4,80,256]{4,3,2,1,0:T(8,128)(2,1)S(1)} %get-tuple-element.13.refs_1_, ...), custom_call_target="tpu_custom_call" | custom-call | tf_op jit(solution)/shard_map/pallas_call | solution.py:659
